TPU v7x, 32 devices: a whole 2x2x4 slice. The times are simulated.
32 devices in a mesh: dp: 16 (over z, y, core), tensor: 2 (over x).
Axes of the slice: x: 2, y: 2, z: 4, core: 2. Of those that a mesh axis runs over, the one named last changes fastest.
Arguments:
- inputs: bfloat16 [64, 288, 768], P('dp'), may hold values from -32 to 32
- memory: bfloat16 [64, 1024, 768], P('dp'), may hold values from -8 to 8
- dec_segments: int32 [64, 288], P('dp'), may hold values from 0 to 3, as said below
- mem_segments: int32 [64, 1024], P('dp'), may hold values from 0 to 3, as said below
- mem_lengths: int32 [64], P('dp'), may hold values from 512 to 1024, as said below
- buckets: int32 [288], replicated, may hold values from 0 to 31, as said below
- cotangent: bfloat16 [64, 288, 768], P('dp'), may hold values from -8 to 8
- attention_in: float32 [768, 6, 768], P('dp', None, 'tensor'), may hold values from -4 to 4
- attention_out: float32 [768, 2, 768], P('dp', None, 'tensor'), may hold values from -4 to 4
- expand_weight: float32 [768, 3072], P('dp', 'tensor'), may hold values from -4 to 4
- contract_weight: float32 [768, 3072], P('dp', 'tensor'), may hold values from -4 to 4
- norm_gains: float32 [768, 3], replicated, may hold values from 0.3 to 2.4
- position_bias: float32 [32, 12], P(None, 'tensor'), may hold values from -4 to 4
- moment_attention_in: float32 [768, 6, 768], P('dp', None, 'tensor'), may hold values from -1 to 1
- square_attention_in: float32 [768, 6, 768], P('dp', None, 'tensor'), may hold values from 0 to 1, as said below
- moment_attention_out: float32 [768, 2, 768], P('dp', None, 'tensor'), may hold values from -1 to 1
- square_attention_out: float32 [768, 2, 768], P('dp', None, 'tensor'), may hold values from 0 to 1, as said below
- moment_expand: float32 [768, 3072], P('dp', 'tensor'), may hold values from -1 to 1
- square_expand: float32 [768, 3072], P('dp', 'tensor'), may hold values from 0 to 1, as said below
- moment_contract: float32 [768, 3072], P('dp', 'tensor'), may hold values from -1 to 1
- square_contract: float32 [768, 3072], P('dp', 'tensor'), may hold values from 0 to 1, as said below
- moment_gains: float32 [768, 3], P('dp'), may hold values from -1 to 1
- square_gains: float32 [768, 3], P('dp'), may hold values from 0 to 1, as said below
- moment_bias: float32 [32, 12], P(None, 'tensor'), may hold values from -1 to 1
- square_bias: float32 [32, 12], P(None, 'tensor'), may hold values from 0 to 1, as said below
Outputs:
- output: float32 [64, 288, 768], P(('dp', 'tensor'))
- input_grad: float32 [64, 288, 768], P('dp')
- memory_grad: float32 [64, 1024, 768], P(('dp', 'tensor'))
- grad_norm: float32 [], replicated
- new_moment_attention_in: float32 [768, 6, 768], P('dp', None, 'tensor')
- new_square_attention_in: float32 [768, 6, 768], P('dp', None, 'tensor')
- new_attention_in: float32 [768, 6, 768], P('dp', None, 'tensor')
- new_moment_attention_out: float32 [768, 2, 768], P('dp', None, 'tensor')
- new_square_attention_out: float32 [768, 2, 768], P('dp', None, 'tensor')
- new_attention_out: float32 [768, 2, 768], P('dp', None, 'tensor')
- new_moment_expand: float32 [768, 3072], P('dp', 'tensor')
- new_square_expand: float32 [768, 3072], P('dp', 'tensor')
- new_expand_weight: float32 [768, 3072], P('dp', 'tensor')
- new_moment_contract: float32 [768, 3072], P('dp', 'tensor')
- new_square_contract: float32 [768, 3072], P('dp', 'tensor')
- new_contract_weight: float32 [768, 3072], P('dp', 'tensor')
- new_moment_gains: float32 [768, 3], P('dp')
- new_square_gains: float32 [768, 3], P('dp')
- new_norm_gains: float32 [768, 3], P('dp')
- new_moment_bias: float32 [32, 12], P(None, 'tensor')
- new_square_bias: float32 [32, 12], P(None, 'tensor')
- new_position_bias: float32 [32, 12], P(None, 'tensor')
Inputs may be any that keep to these rules, and one draw needn't show every extreme that they name: `dec_segments`: in every row the ids never fall, start at 0 and end at 3, so each of the 4 documents holds one or more decoder positions. `mem_segments`: in every row the ids never fall and start at 0; memory document s belongs to decoder document s of the same row; every document has one or more positions below the row's mem_lengths entry, and positions at or past it carry 4 - 1. `mem_lengths`: among each device's 4 rows one has length 1024. `buckets`: entry d is d for d < 16, never falls as d grows, and is 31 for d >= 128. `square_attention_in`: Positive. `square_attention_out`: Positive. `square_expand`: Positive. `square_contract`: Positive. `square_gains`: Positive. `square_bias`: Positive.
All inputs are finite; a program needn't handle non-finite values.
Results may differ from a plain program's by a relative error of at most 0.022.
Values may be sent and summed in bfloat16 or wider, within the bound.
No kernel may reach another device: no remote copies, remote signals or barrier semaphores. Data moves between devices by JAX's collectives and lax.ppermute only.
A program may use at most 256 MiB of HBM per device.

v0:
```python
import jax
import jax.numpy as jnp
from jax import lax
from jax.sharding import PartitionSpec as P

DH = 64
STEP = 10


NORM_EPS = 1e-06
MASKED = -1e30
CLIP_NORM = 1.0
BETA_ONE = 0.9
BETA_TWO = 0.95
ADAM_EPS = 1e-08
MATRIX_RATE = 0.08
SMALL_RATE = 0.8
DECAY_RATE = 0.1
GELU_SCALE = 0.7978845608028654
GELU_CUBIC = 0.044715


def gelu_tanh(values):
    return (
        0.5
        * values
        * (1.0 + jnp.tanh(GELU_SCALE * (values + GELU_CUBIC * values * values * values)))
    )


def norm_scale(hidden):
    return lax.rsqrt(jnp.mean(hidden * hidden, axis=-1, keepdims=True) + NORM_EPS)


def norm_back(hidden, factor, gain_column, upstream):
    weighted = upstream * gain_column
    inner_mean = jnp.mean(weighted * hidden, axis=-1, keepdims=True)
    return factor * weighted - factor * factor * factor * hidden * inner_mean


def gain_slope(hidden, factor, upstream):
    return jnp.sum(upstream * hidden * factor, axis=(0, 1))


def split_heads(values):
    return values.reshape(values.shape[:-1] + (values.shape[-1] // DH, DH))


def join_heads(values):
    return values.reshape(values.shape[:-2] + (values.shape[-2] * values.shape[-1],))


def in_pairs(values):
    return values.reshape((values.shape[0] // 2, 2) + values.shape[1:])


def from_pairs(values):
    return values.reshape((values.shape[0] * values.shape[1],) + values.shape[2:])


def lower_toeplitz(table):
    channels, length = table.shape
    padded = jnp.concatenate([jnp.zeros((channels, length - 1), table.dtype), table], axis=1)
    flipped = jnp.concatenate([padded[:, ::-1], jnp.zeros((channels, 1), table.dtype)], axis=1)
    tiled = jnp.broadcast_to(flipped[:, None, :], (channels, length, 2 * length))
    flat = tiled.reshape(channels, length * 2 * length)[:, : length * (2 * length - 1)]
    return flat.reshape(channels, length, 2 * length - 1)[:, :, length - 1 : 2 * length - 1]


def masked_scores(queries, keys_in, extra_bias, allowed):
    scores = (
        jnp.einsum("rqhd,rkhd->rhqk", queries, keys_in, preferred_element_type=jnp.float32)
        + extra_bias
    )
    return jnp.where(allowed, scores, MASKED)


def attend_forward(queries, keys_in, values_in, extra_bias, allowed):
    scores = masked_scores(queries, keys_in, extra_bias, allowed)
    row_max = jnp.max(scores, axis=-1, keepdims=True)
    exponent = jnp.exp(scores - row_max)
    summed = jnp.sum(exponent, axis=-1, keepdims=True)
    weights = (exponent / summed).astype(jnp.bfloat16)
    mixture = jnp.einsum("rhqk,rkhd->rqhd", weights, values_in, preferred_element_type=jnp.float32)
    return (mixture.astype(jnp.bfloat16), row_max + jnp.log(summed))


def attend_backward(queries, keys_in, values_in, extra_bias, allowed, logsum, upstream):
    scores = masked_scores(queries, keys_in, extra_bias, allowed)
    probabilities = jnp.exp(scores - logsum)
    weights = probabilities.astype(jnp.bfloat16)
    slope_probs = jnp.einsum(
        "rqhd,rkhd->rhqk", upstream, values_in, preferred_element_type=jnp.float32
    )
    centered = slope_probs - jnp.sum(slope_probs * probabilities, axis=-1, keepdims=True)
    scores_gradient = (probabilities * centered).astype(jnp.bfloat16)
    slope_queries = jnp.einsum(
        "rhqk,rkhd->rqhd", scores_gradient, keys_in, preferred_element_type=jnp.float32
    ).astype(jnp.bfloat16)
    slope_keys = jnp.einsum(
        "rhqk,rqhd->rkhd", scores_gradient, queries, preferred_element_type=jnp.float32
    ).astype(jnp.bfloat16)
    slope_values = jnp.einsum(
        "rhqk,rqhd->rkhd", weights, upstream, preferred_element_type=jnp.float32
    ).astype(jnp.bfloat16)
    return (slope_queries, slope_keys, slope_values, scores_gradient)


def adam_update(weight, gradient, moment, square, learn_rate, weight_decay):
    new_moment = BETA_ONE * moment + (1.0 - BETA_ONE) * gradient
    new_square = BETA_TWO * square + (1.0 - BETA_TWO) * gradient * gradient
    direction = (
        new_moment
        / (1.0 - BETA_ONE**STEP)
        / (jnp.sqrt(new_square / (1.0 - BETA_TWO**STEP)) + ADAM_EPS)
    )
    return (new_moment, new_square, weight - learn_rate * (direction + weight_decay * weight))


def on_device(
    inputs,
    memory,
    dec_segments,
    mem_segments,
    mem_lengths,
    buckets,
    cotangent,
    attention_in,
    attention_out,
    expand_weight,
    contract_weight,
    norm_gains,
    position_bias,
    moment_attention_in,
    square_attention_in,
    moment_attention_out,
    square_attention_out,
    moment_expand,
    square_expand,
    moment_contract,
    square_contract,
    moment_gains,
    square_gains,
    moment_bias,
    square_bias,
):
    tensor_count = lax.axis_size("tensor")
    tensor_index = lax.axis_index("tensor")
    data_index = lax.axis_index("dp")
    gathered = (
        lax.all_gather(attention_in.astype(jnp.bfloat16), "dp", axis=0, tiled=True),
        lax.all_gather(attention_out.astype(jnp.bfloat16), "dp", axis=0, tiled=True),
        lax.all_gather(expand_weight.astype(jnp.bfloat16), "dp", axis=0, tiled=True),
        lax.all_gather(contract_weight.astype(jnp.bfloat16), "dp", axis=0, tiled=True),
    )
    input_kernel_list, out_kernels, up_kernel, down_kernel = gathered
    row_count, length = (inputs.shape[0], inputs.shape[1])
    row_share = row_count // tensor_count
    own_start = tensor_index * row_share
    hidden_zero = inputs.astype(jnp.float32)
    scale_zero = norm_scale(hidden_zero)
    first_normalized = (hidden_zero * scale_zero * norm_gains[:, 0]).astype(jnp.bfloat16)
    self_head_split = jnp.einsum(
        "nmq,qfw->fnmw",
        first_normalized,
        input_kernel_list[:, 0:3],
        preferred_element_type=jnp.float32,
    ).astype(jnp.bfloat16)
    self_query, self_key, self_value = (
        split_heads(self_head_split[0]),
        split_heads(self_head_split[1]),
        split_heads(self_head_split[2]),
    )
    positions = jnp.arange(length, dtype=jnp.int32)
    distance = positions[:, None] - positions[None, :]
    causal = distance >= 0
    bucket_table = (
        buckets[None, :] == jnp.arange(position_bias.shape[0], dtype=jnp.int32)[:, None]
    ).astype(jnp.float32)
    bucket_grid = lower_toeplitz(bucket_table)
    self_extra = jnp.einsum(
        "gzp,gm->mzp",
        bucket_grid,
        position_bias,
        precision=lax.Precision.HIGHEST,
        preferred_element_type=jnp.float32,
    )[None]
    self_allowed = (causal[None] & (dec_segments[:, :, None] == dec_segments[:, None, :]))[:, None]
    self_mixed, self_logsum = attend_forward(
        self_query, self_key, self_value, self_extra, self_allowed
    )
    self_flat = join_heads(self_mixed)
    self_term = jnp.einsum(
        "rle,de->rld", self_flat, out_kernels[:, 0], preferred_element_type=jnp.float32
    )
    hidden_one = hidden_zero + lax.psum(self_term, "tensor")
    scale_one = norm_scale(hidden_one)
    normed_one = (hidden_one * scale_one * norm_gains[:, 1]).astype(jnp.bfloat16)
    cross_query = split_heads(
        jnp.einsum(
            "rld,de->rle", normed_one, input_kernel_list[:, 3], preferred_element_type=jnp.float32
        ).astype(jnp.bfloat16)
    )
    memory_head_split = jnp.einsum(
        "oah,hjy->joay", memory, input_kernel_list[:, 4:6], preferred_element_type=jnp.float32
    ).astype(jnp.bfloat16)
    cross_key, cross_value = (split_heads(memory_head_split[0]), split_heads(memory_head_split[1]))
    key_index = jnp.arange(memory.shape[1], dtype=jnp.int32)

    def cross_allowed(decoder_ids, memory_ids, lengths_part):
        same_doc = decoder_ids[:, :, None] == memory_ids[:, None, :]
        live_keys = key_index[None, None, :] < lengths_part[:, None, None]
        return (same_doc & live_keys)[:, None]

    def cross_forward(pieces):
        return attend_forward(
            pieces[0], pieces[1], pieces[2], 0.0, cross_allowed(pieces[3], pieces[4], pieces[5])
        )

    cross_pieces = tuple(
        (
            in_pairs(member)
            for member in (
                cross_query,
                cross_key,
                cross_value,
                dec_segments,
                mem_segments,
                mem_lengths,
            )
        )
    )
    cross_mixed, cross_logsum = lax.map(cross_forward, cross_pieces)
    cross_flat = join_heads(from_pairs(cross_mixed))
    cross_term = jnp.einsum(
        "rle,de->rld", cross_flat, out_kernels[:, 1], preferred_element_type=jnp.float32
    )
    hidden_two = hidden_one + lax.psum(cross_term.astype(jnp.bfloat16), "tensor").astype(
        jnp.float32
    )
    scale_two = norm_scale(hidden_two)
    normed_two = (hidden_two * scale_two * norm_gains[:, 2]).astype(jnp.bfloat16)
    preactivation = jnp.einsum(
        "rld,df->rlf", normed_two, up_kernel, preferred_element_type=jnp.float32
    )
    activated, gelu_pullback = jax.vjp(gelu_tanh, preactivation)
    activated_low = activated.astype(jnp.bfloat16)
    segment_rows = activated_low
    feed_sum = lax.psum_scatter(
        jnp.einsum(
            "rlf,df->rld", segment_rows, down_kernel, preferred_element_type=jnp.float32
        ).astype(jnp.bfloat16),
        "tensor",
        scatter_dimension=0,
        tiled=True,
    ).astype(jnp.float32)
    output = lax.dynamic_slice_in_dim(hidden_two, own_start, row_share, 0) + feed_sum
    slope_down = jnp.einsum(
        "rlf,rld->df", activated_low, cotangent, preferred_element_type=jnp.float32
    )
    slope_activated = jnp.einsum(
        "rld,df->rlf", cotangent, down_kernel, preferred_element_type=jnp.float32
    )
    slope_pre = gelu_pullback(slope_activated)[0].astype(jnp.bfloat16)
    slope_up = jnp.einsum("rld,rlf->df", normed_two, slope_pre, preferred_element_type=jnp.float32)
    normed_slope_two = lax.psum(
        jnp.einsum("rlf,df->rld", slope_pre, up_kernel, preferred_element_type=jnp.float32),
        "tensor",
    )
    gain_two = gain_slope(hidden_two, scale_two, normed_slope_two)
    slope_two = cotangent.astype(jnp.float32) + norm_back(
        hidden_two, scale_two, norm_gains[:, 2], normed_slope_two
    )
    cross_upstream = slope_two.astype(jnp.bfloat16)
    slope_out_cross = jnp.einsum(
        "rld,rle->de", cross_upstream, cross_flat, preferred_element_type=jnp.float32
    )
    slope_cross_flat = jnp.einsum(
        "rld,de->rle", cross_upstream, out_kernels[:, 1], preferred_element_type=jnp.float32
    ).astype(jnp.bfloat16)

    def cross_backward(pieces):
        outcome = attend_backward(
            pieces[0],
            pieces[1],
            pieces[2],
            0.0,
            cross_allowed(pieces[3], pieces[4], pieces[5]),
            pieces[6],
            pieces[7],
        )
        return (outcome[0], outcome[1], outcome[2])

    cross_slopes = lax.map(
        cross_backward, cross_pieces + (cross_logsum, in_pairs(split_heads(slope_cross_flat)))
    )
    slope_cross_query, slope_cross_key, slope_cross_value = (
        join_heads(from_pairs(member)) for member in cross_slopes
    )
    memory_gradient_list = jnp.stack([slope_cross_key, slope_cross_value])
    slope_in_query = jnp.einsum(
        "rld,rle->de", normed_one, slope_cross_query, preferred_element_type=jnp.float32
    )
    slope_in_memory = jnp.einsum(
        "gwz,agwp->zap", memory, memory_gradient_list, preferred_element_type=jnp.float32
    )
    segment_rows = memory_gradient_list
    memory_grad = lax.psum_scatter(
        jnp.einsum(
            "iuto,wio->utw",
            segment_rows,
            input_kernel_list[:, 4:6],
            preferred_element_type=jnp.float32,
        ).astype(jnp.bfloat16),
        "tensor",
        scatter_dimension=0,
        tiled=True,
    ).astype(jnp.float32)
    normed_slope_one = lax.psum(
        jnp.einsum(
            "rle,de->rld",
            slope_cross_query,
            input_kernel_list[:, 3],
            preferred_element_type=jnp.float32,
        ).astype(jnp.bfloat16),
        "tensor",
    ).astype(jnp.float32)
    gain_one = gain_slope(hidden_one, scale_one, normed_slope_one)
    slope_one = slope_two + norm_back(hidden_one, scale_one, norm_gains[:, 1], normed_slope_one)
    self_upstream = slope_one.astype(jnp.bfloat16)
    slope_out_self = jnp.einsum(
        "rld,rle->de", self_upstream, self_flat, preferred_element_type=jnp.float32
    )
    slope_self_flat = jnp.einsum(
        "rld,de->rle", self_upstream, out_kernels[:, 0], preferred_element_type=jnp.float32
    ).astype(jnp.bfloat16)
    slope_sq, slope_sk, slope_sv, scores_gradient = attend_backward(
        self_query,
        self_key,
        self_value,
        self_extra,
        self_allowed,
        self_logsum,
        split_heads(slope_self_flat),
    )
    bucket_lookup_grid = bucket_grid.astype(jnp.bfloat16)
    bias_local = jnp.einsum(
        "gzp,xmzp->gm", bucket_lookup_grid, scores_gradient, preferred_element_type=jnp.float32
    )
    self_gradient_list = jnp.stack(
        [join_heads(slope_sq), join_heads(slope_sk), join_heads(slope_sv)]
    )
    slope_in_self = jnp.einsum(
        "oap,moai->pmi", first_normalized, self_gradient_list, preferred_element_type=jnp.float32
    )
    normed_slope_zero = lax.psum(
        jnp.einsum(
            "qxbp,uqp->xbu",
            self_gradient_list,
            input_kernel_list[:, 0:3],
            preferred_element_type=jnp.float32,
        ).astype(jnp.bfloat16),
        "tensor",
    ).astype(jnp.float32)
    gain_zero = gain_slope(hidden_zero, scale_zero, normed_slope_zero)
    input_grad = slope_one + norm_back(hidden_zero, scale_zero, norm_gains[:, 0], normed_slope_zero)
    slope_in = jnp.concatenate([slope_in_self, slope_in_query[:, None], slope_in_memory], axis=1)
    slope_out = jnp.stack([slope_out_self, slope_out_cross], axis=1)
    gain_slopes = jnp.stack([gain_zero, gain_one, gain_two], axis=1)
    shared_in, shared_out, shared_up, shared_down, shared_gains = (
        lax.psum_scatter(slope_in, "dp", scatter_dimension=0, tiled=True),
        lax.psum_scatter(slope_out, "dp", scatter_dimension=0, tiled=True),
        lax.psum_scatter(slope_up, "dp", scatter_dimension=0, tiled=True),
        lax.psum_scatter(slope_down, "dp", scatter_dimension=0, tiled=True),
        lax.psum_scatter(gain_slopes, "dp", scatter_dimension=0, tiled=True),
    )
    heads_local = position_bias.shape[1]
    bias_slopes = jnp.zeros((position_bias.shape[0], heads_local * tensor_count), jnp.float32)
    bias_slopes = lax.dynamic_update_slice_in_dim(
        bias_slopes, bias_local, tensor_index * heads_local, 1
    )
    gain_square = jnp.where(tensor_index == 0, jnp.sum(shared_gains * shared_gains), 0.0)
    local_square = (
        jnp.sum(shared_in * shared_in)
        + jnp.sum(shared_out * shared_out)
        + jnp.sum(shared_up * shared_up)
        + jnp.sum(shared_down * shared_down)
        + gain_square
    )
    square_sum, bias_summed = lax.psum((local_square, bias_slopes), ("dp", "tensor"))
    grad_norm = jnp.sqrt(square_sum + jnp.sum(bias_summed * bias_summed))
    clip_factor = jnp.minimum(1.0, CLIP_NORM / (grad_norm + 1e-06))
    bias_share = lax.dynamic_slice_in_dim(bias_summed, tensor_index * heads_local, heads_local, 1)
    gain_rows = shared_gains.shape[0]
    old_gains = lax.dynamic_slice_in_dim(norm_gains, data_index * gain_rows, gain_rows, 0)
    new_moment_attention_in, new_square_attention_in, new_attention_in = adam_update(
        attention_in,
        shared_in * clip_factor,
        moment_attention_in,
        square_attention_in,
        MATRIX_RATE,
        DECAY_RATE,
    )
    new_moment_attention_out, new_square_attention_out, new_attention_out = adam_update(
        attention_out,
        shared_out * clip_factor,
        moment_attention_out,
        square_attention_out,
        MATRIX_RATE,
        DECAY_RATE,
    )
    new_moment_expand, new_square_expand, new_expand_weight = adam_update(
        expand_weight,
        shared_up * clip_factor,
        moment_expand,
        square_expand,
        MATRIX_RATE,
        DECAY_RATE,
    )
    new_moment_contract, new_square_contract, new_contract_weight = adam_update(
        contract_weight,
        shared_down * clip_factor,
        moment_contract,
        square_contract,
        MATRIX_RATE,
        DECAY_RATE,
    )
    new_moment_gains, new_square_gains, new_norm_gains = adam_update(
        old_gains, shared_gains * clip_factor, moment_gains, square_gains, SMALL_RATE, 0.0
    )
    new_moment_bias, new_square_bias, new_position_bias = adam_update(
        position_bias, bias_share * clip_factor, moment_bias, square_bias, SMALL_RATE, 0.0
    )
    return (
        output,
        input_grad,
        memory_grad,
        grad_norm,
        new_moment_attention_in,
        new_square_attention_in,
        new_attention_in,
        new_moment_attention_out,
        new_square_attention_out,
        new_attention_out,
        new_moment_expand,
        new_square_expand,
        new_expand_weight,
        new_moment_contract,
        new_square_contract,
        new_contract_weight,
        new_moment_gains,
        new_square_gains,
        new_norm_gains,
        new_moment_bias,
        new_square_bias,
        new_position_bias,
    )


def solution(mesh):
    return jax.shard_map(
        on_device,
        mesh=mesh,
        in_specs=(
            P("dp", None, None),
            P("dp", None, None),
            P("dp", None),
            P("dp", None),
            P("dp"),
            P(),
            P("dp", None, None),
            P("dp", None, "tensor"),
            P("dp", None, "tensor"),
            P("dp", "tensor"),
            P("dp", "tensor"),
            P(),
            P(None, "tensor"),
            P("dp", None, "tensor"),
            P("dp", None, "tensor"),
            P("dp", None, "tensor"),
            P("dp", None, "tensor"),
            P("dp", "tensor"),
            P("dp", "tensor"),
            P("dp", "tensor"),
            P("dp", "tensor"),
            P("dp", None),
            P("dp", None),
            P(None, "tensor"),
            P(None, "tensor"),
        ),
        out_specs=(
            P(("dp", "tensor"), None, None),
            P("dp", None, None),
            P(("dp", "tensor"), None, None),
            P(),
            P("dp", None, "tensor"),
            P("dp", None, "tensor"),
            P("dp", None, "tensor"),
            P("dp", None, "tensor"),
            P("dp", None, "tensor"),
            P("dp", None, "tensor"),
            P("dp", "tensor"),
            P("dp", "tensor"),
            P("dp", "tensor"),
            P("dp", "tensor"),
            P("dp", "tensor"),
            P("dp", "tensor"),
            P("dp", None),
            P("dp", None),
            P("dp", None),
            P(None, "tensor"),
            P(None, "tensor"),
            P(None, "tensor"),
        ),
        check_vma=False,
    )
```

profile of v0, /device:TPU:0, one launch (start us, length us, event | category | flops | bytes accessed | tf_op | source)
XLA Modules:
  0.0 1342.2 jit_solution(15040165948285591371)
XLA Ops:
  15.9 9.5 broadcast_in_dim.74
  25.5 31.4 %reshape.253 = f32[32,165888]{1,0:T(8,128)} reshape(f32[32,288,576]{2,1,0:T(8,128)} %broadcast_in_dim.74) | data formatting | bytes 42467328 | tf_op jit(solution)/shard_map/reshape | solution.py:66
  56.9 15.9 %slice.72 = f32[32,165600]{1,0:T(8,128)} slice(f32[32,165888]{1,0:T(8,128)} %reshape.253), slice={[0:32], [0:165600]} | slice | bytes 42393600 | tf_op jit(solution)/shard_map/slice | solution.py:66
  72.9 44.6 %reshape.254 = f32[32,288,575]{2,1,0:T(8,128)} reshape(f32[32,165600]{1,0:T(8,128)} %slice.72) | data formatting | bytes 42393600 | tf_op jit(solution)/shard_map/reshape | solution.py:67
  117.5 13.9 %slice.73 = f32[32,288,288]{2,1,0:T(8,128)} slice(f32[32,288,575]{2,1,0:T(8,128)} %reshape.254), slice={[0:32], [0:288], [287:575]} | slice | bytes 21233664 | tf_op jit(solution)/shard_map/slice | solution.py:67
  131.4 20.4 %fusion.115 = f32[6,288,288]{2,0,1:T(8,128)} fusion(f32[32,288,288]{2,1,0:T(8,128)} %slice.73, f32[32,6]{0,1:T(8,128)S(1)} %copy-done.71), kind=kOutput, calls=%fused_computation.154 | convolution fusion | flops 191102976 | bytes 12608256 | tf_op jit(solution)/shard_map/gzp,gm->mzp/dot_general | solution.py:181
  168.7 8.4 fusion.161
  202.8 86.8 %all-reduce.9.cloned.1.call-done = f32[4,288,768]{2,1,0:T(8,128)} async-done(((f32[4,288,768]{2,1,0:T(8,128)}), f32[4,288,768]{2,1,0:T(8,128)}) %all-reduce.9.cloned.1.call-update) | async-done | bytes 3538960 | tf_op jit(solution)/shard_map/psum | solution.py:196
  301.1 26.4 %while.28 = (s32[]{:T(128)}, bf16[2,2,288,6,64]{2,4,3,1,0:T(8,128)(2,1)}, f32[2,2,6,288,1]{3,2,1,4,0:T(8,128)S(1)}, bf16[2,2,1024,6,64]{2,4,3,1,0:T(8,128)(2,1)}...) while((s32[]{:T(128)}, ...), condition=%wide.region_8.9_spmd.clone, body=%wide.region_5.8_spmd.clone.sunk | while | flops 939219584 | bytes 69015016 | solution.py:233
  334.1 53.4 %all-reduce.11.cloned.1.call-done = bf16[4,288,768]{2,1,0:T(8,128)(2,1)} async-done(((bf16[4,288,768]{2,1,0:T(8,128)(2,1)}), bf16[4,288,768]{2,1,0:T(8,128)(2,1)}) %all-reduce.11.cloned.1.call-update) | async-done | bytes 1769488 | tf_op jit(solution)/shard_map/psum | solution.py:238
  392.3 40.1 %all-gather.9.cloned.1.call-done = bf16[768,1536]{1,0:T(8,128)(2,1)} async-done(((bf16[48,1536]{1,0:T(8,128)(2,1)}), bf16[768,1536]{1,0:T(8,128)(2,1)}) %all-gather.9.cloned.1.call-update) | async-done | bytes 2359312 | tf_op jit(solution)/shard_map/all_gather | solution.py:153
  432.4 8.5 fusion.113
  441.0 35.2 %all-gather.11.cloned.1.call-done = bf16[768,1536]{1,0:T(8,128)(2,1)} async-done(((bf16[48,1536]{1,0:T(8,128)(2,1)}), bf16[768,1536]{1,0:T(8,128)(2,1)}) %all-gather.11.cloned.1.call-update) | async-done | bytes 2359312 | tf_op jit(solution)/shard_map/all_gather | solution.py:154
  476.2 10.5 fusion.77
  493.3 93.2 %all-reduce.13.cloned.1.call-done = f32[4,288,768]{2,1,0:T(8,128)} async-done(((f32[4,288,768]{2,1,0:T(8,128)}), f32[4,288,768]{2,1,0:T(8,128)}) %all-reduce.13.cloned.1.call-update) | async-done | bytes 3538960 | tf_op jit(solution)/shard_map/psum | solution.py:266
  601.0 69.6 %while.29 = (s32[]{:T(128)}, bf16[2,2,288,6,64]{2,4,3,1,0:T(8,128)(2,1)}, bf16[2,2,1024,6,64]{2,4,3,1,0:T(8,128)(2,1)}, bf16[2,2,1024,6,64]{2,4,3,1,0:T(8,128)(2...) while((s32[]{:T(128)}, ...), condition=%wide.region_16.17_spmd.clone, body=%wide.region_14.16_spmd.clone.sunk | while | flops 2310363648 | bytes 188706512 | solution.py:294
  611.9 9.2 multiply_reduce_fusion.13
  646.6 9.2 multiply_reduce_fusion.13
  676.3 54.3 %all-reduce.15.cloned.1.call-done = bf16[4,288,768]{2,1,0:T(8,128)(2,1)} async-done(((bf16[4,288,768]{2,1,0:T(8,128)(2,1)}), bf16[4,288,768]{2,1,0:T(8,128)(2,1)}) %all-reduce.15.cloned.1.call-update) | async-done | bytes 1769488 | tf_op jit(solution)/shard_map/psum | solution.py:319
  785.2 9.2 fusion.119
  794.4 9.1 convolution_bitcast_fusion
  819.5 21.5 %all-reduce.17.cloned.1.call-done = bf16[4,288,768]{2,1,0:T(8,128)(2,1)} async-done(((bf16[4,288,768]{2,1,0:T(8,128)(2,1)}), bf16[4,288,768]{2,1,0:T(8,128)(2,1)}) %all-reduce.17.cloned.1.call-update) | async-done | bytes 1769488 | tf_op jit(solution)/shard_map/psum | solution.py:356
  863.4 9.0 fusion.122
  878.6 9.5 bitcast_convert_fusion
  894.5 13.5 %fusion.132 = f32[32,6]{0,1:T(8,128)S(1)} fusion(bf16[6,288,288]{2,0,1:T(8,128)(2,1)} %copy.154, f32[32,288,288]{2,1,0:T(8,128)} %slice.73), kind=kOutput, calls=%fused_computation.177 | convolution fusion | flops 31850496 | bytes 11612928 | tf_op jit(solution)/shard_map/gzp,xmzp->gm/dot_general | solution.py:347
  909.9 41.6 %reduce-scatter.20.cloned.1.call-done = f32[48,1536]{1,0:T(8,128)} async-done(((f32[768,1536]{1,0:T(8,128)}), f32[48,1536]{1,0:T(8,128)}) %reduce-scatter.20.cloned.1.call-update) | async-done | bytes 294928 | tf_op jit(solution)/shard_map/reduce_scatter | solution.py:374
  953.2 77.1 %reduce-scatter.18.cloned.1.call-done = f32[48,1536]{1,0:T(8,128)} async-done(((f32[768,1536]{1,0:T(8,128)}), f32[48,1536]{1,0:T(8,128)}) %reduce-scatter.18.cloned.1.call-update) | async-done | bytes 294928 | tf_op jit(solution)/shard_map/reduce_scatter | solution.py:373
  1033.3 55.8 %reduce-scatter.22.cloned.1.call-done = f32[48,3]{1,0:T(8,128)} async-done(((f32[768,3]{1,0:T(8,128)}), f32[48,3]{1,0:T(8,128)}) %reduce-scatter.22.cloned.1.call-update) | async-done | bytes 592
  1091.2 64.0 %reduce-scatter.16.cloned.1.call-done = f32[48,2,384]{2,0,1:T(8,128)} async-done(((f32[768,2,384]{2,0,1:T(8,128)}), f32[48,2,384]{2,0,1:T(8,128)}) %reduce-scatter.16.cloned.1.call-update) | async-done | bytes 147472 | tf_op jit(solution)/shard_map/reduce_scatter | solution.py:372
  1156.8 91.4 %reduce-scatter.14.cloned.1.call-done = f32[48,6,384]{2,0,1:T(8,128)} async-done(((f32[768,6,384]{2,0,1:T(8,128)}), f32[48,6,384]{2,0,1:T(8,128)}) %reduce-scatter.14.cloned.1.call-update) | async-done | bytes 442384 | tf_op jit(solution)/shard_map/reduce_scatter | solution.py:371
  1256.6 41.0 %all-reduce.2 = (f32[]{:T(128)}, f32[32,12]{0,1:T(8,128)S(1)}) all-reduce(f32[]{:T(128)S(6)} %add.259, f32[32,12]{0,1:T(8,128)} %dynamic_update_slice.21), channel_id=1, replica_groups=mesh['dp'=16,'tensor'=2] {'dp','tensor'}, use_global_device_ids=true, to_apply=%region_36.37 | all-reduce | flops 385 | bytes 3080 | tf_op jit(solution)/shard_map/psum | solution.py:390
  1310.0 19.0 %reduce-scatter.12.cloned.1.call-done = bf16[2,1024,768]{2,1,0:T(8,128)(2,1)} async-done(((bf16[4,1024,768]{2,1,0:T(8,128)(2,1)}), bf16[2,1024,768]{2,1,0:T(8,128)(2,1)}) %reduce-scatter.12.cloned.1.call-update) | async-done | bytes 3145744 | tf_op jit(solution)/shard_map/reduce_scatter | solution.py:308
  (361 shorter events, 313.9 us)
Async XLA Ops:
  7.2 151.1 %all-gather.5.cloned.1.call-start = ((), (), s32[]{:S(2)}) async-start(), calls=%async_computation.7 | async-start | bytes 3760128 | tf_op jit(solution)/shard_map/all_gather | solution.py:151
  9.0 178.6 %all-gather.7.cloned.1.call-start = ((), (), s32[]{:S(2)}) async-start(), calls=%async_computation.8 | async-start | bytes 1253376 | tf_op jit(solution)/shard_map/all_gather | solution.py:152
  10.6 279.0 %all-reduce.9.cloned.1.call-start = ((), (), s32[]{:S(2)}) async-start(), calls=%async_computation.9 | async-start | bytes 7077888 | tf_op jit(solution)/shard_map/psum | solution.py:196
  13.2 145.1 %copy-start.59 = (f32[4,288]{1,0:T(4,128)}, f32[4,288]{1,0:T(4,128)S(1)}, u32[]{:S(2)}) copy-start(f32[4,288]{1,0:T(4,128)S(1)} %get-tuple-element.369) | copy-start | bytes 13828
  15.4 143.0 %copy-start.65 = (f32[768]{0:T(1024)}, f32[768]{0:T(1024)S(1)}, u32[]{:S(2)}) copy-start(f32[768]{0:T(1024)S(1)} %get-tuple-element.290) | copy-start | bytes 9220
  15.4 278.0 %copy-start.55 = (f32[768]{0:T(1024)}, f32[768]{0:T(1024)S(1)}, u32[]{:S(2)}) copy-start(f32[768]{0:T(1024)S(1)} %get-tuple-element.289) | copy-start | bytes 9220
  192.2 195.3 %all-reduce.11.cloned.1.call-start = ((), (), s32[]{:S(2)}) async-start(), calls=%async_computation.10 | async-start | bytes 3538944 | tf_op jit(solution)/shard_map/psum | solution.py:238
  331.5 100.9 %all-gather.9.cloned.1.call-start = ((), (), s32[]{:S(2)}) async-start(), calls=%async_computation.11 | async-start | bytes 2506752 | tf_op jit(solution)/shard_map/all_gather | solution.py:153
  332.3 143.9 %all-gather.11.cloned.1.call-start = ((), (), s32[]{:S(2)}) async-start(), calls=%async_computation.12 | async-start | bytes 2506752 | tf_op jit(solution)/shard_map/all_gather | solution.py:154
  334.0 98.4 %copy-start.46 = (f32[768]{0:T(1024)S(1)}, f32[768]{0:T(1024)}, u32[]{:S(2)}) copy-start(f32[768]{0:T(1024)} %get-tuple-element.288) | copy-start | bytes 9220
  334.0 252.5 %all-reduce.13.cloned.1.call-start = ((), (), s32[]{:S(2)}) async-start(), calls=%async_computation.14 | async-start | bytes 7077888 | tf_op jit(solution)/shard_map/psum | solution.py:266
  392.3 199.0 %copy-start.43 = (f32[4,288]{1,0:T(4,128)}, f32[4,288]{1,0:T(4,128)S(1)}, u32[]{:S(2)}) copy-start(f32[4,288]{1,0:T(4,128)S(1)} %get-tuple-element.373) | copy-start | bytes 13828
  392.3 199.0 %copy-start.62 = (f32[4,288]{1,0:T(4,128)}, f32[4,288]{1,0:T(4,128)S(1)}, u32[]{:S(2)}) copy-start(f32[4,288]{1,0:T(4,128)S(1)} %get-tuple-element.372) | copy-start | bytes 13828
  493.3 237.3 %all-reduce.15.cloned.1.call-start = ((), (), s32[]{:S(2)}) async-start(), calls=%async_computation.15 | async-start | bytes 3538944 | tf_op jit(solution)/shard_map/psum | solution.py:319
  670.7 59.9 %copy-start.56 = (f32[768]{0:T(1024)S(1)}, f32[768]{0:T(1024)}, u32[]{:S(2)}) copy-start(f32[768]{0:T(1024)} %copy-done.55) | copy-start | bytes 9220
  674.6 60.6 %copy-start.6 = (f32[4,288,768]{2,1,0:T(8,128)S(1)}, f32[4,288,768]{2,1,0:T(8,128)}, u32[]{:S(2)}) copy-start(f32[4,288,768]{2,1,0:T(8,128)} %get-tuple-element.356) | copy-start | bytes 10616836
  674.6 60.6 %copy-start.44 = (f32[4,288]{1,0:T(4,128)S(1)}, f32[4,288]{1,0:T(4,128)}, u32[]{:S(2)}) copy-start(f32[4,288]{1,0:T(4,128)} %copy-done.43) | copy-start | bytes 13828
  674.6 60.6 %copy-start.47 = (f32[768]{0:T(1024)S(1)}, f32[768]{0:T(1024)}, u32[]{:S(2)}) copy-start(f32[768]{0:T(1024)} %get-tuple-element.288) | copy-start | bytes 9220
  674.6 166.4 %all-reduce.17.cloned.1.call-start = ((), (), s32[]{:S(2)}) async-start(), calls=%async_computation.16 | async-start | bytes 3538944 | tf_op jit(solution)/shard_map/psum | solution.py:356
  785.1 103.0 %reduce-scatter.10.cloned.1.call-start = ((), (), s32[]{:S(2)}) async-start(), calls=%async_computation.13 | async-start | bytes 2654208 | tf_op jit(solution)/shard_map/reduce_scatter | solution.py:249
  794.4 157.2 %reduce-scatter.20.cloned.1.call-start = ((), (), s32[]{:S(2)}) async-start(), calls=%async_computation.21 | async-start | bytes 5013504 | tf_op jit(solution)/shard_map/reduce_scatter | solution.py:374
  803.6 226.8 %reduce-scatter.18.cloned.1.call-start = ((), (), s32[]{:S(2)}) async-start(), calls=%async_computation.20 | async-start | bytes 5013504 | tf_op jit(solution)/shard_map/reduce_scatter | solution.py:373
  810.7 278.4 %reduce-scatter.22.cloned.1.call-start = ((), (), s32[]{:S(2)}) async-start(), calls=%async_computation.22 | async-start | bytes 417792
  846.2 309.0 %reduce-scatter.16.cloned.1.call-start = ((), (), s32[]{:S(2)}) async-start(), calls=%async_computation.19 | async-start | bytes 2506752 | tf_op jit(solution)/shard_map/reduce_scatter | solution.py:372
  849.5 398.7 %reduce-scatter.14.cloned.1.call-start = ((), (), s32[]{:S(2)}) async-start(), calls=%async_computation.18 | async-start | bytes 7520256 | tf_op jit(solution)/shard_map/reduce_scatter | solution.py:371
  878.5 450.5 %reduce-scatter.12.cloned.1.call-start = ((), (), s32[]{:S(2)}) async-start(), calls=%async_computation.17 | async-start | bytes 9437184 | tf_op jit(solution)/shard_map/reduce_scatter | solution.py:308
  894.5 358.0 %copy-start.13 = (f32[4,288,768]{2,1,0:T(8,128)S(1)}, f32[4,288,768]{2,1,0:T(8,128)}, u32[]{:S(2)}) copy-start(f32[4,288,768]{2,1,0:T(8,128)} %copy-done.11) | copy-start | bytes 10616836
  1256.5 52.0 %copy-start.33 = (f32[48,1536]{1,0:T(8,128)S(1)}, f32[48,1536]{1,0:T(8,128)}, u32[]{:S(2)}) copy-start(f32[48,1536]{1,0:T(8,128)} %param.38) | copy-start | bytes 884740
  1256.5 51.9 %copy-start.34 = (f32[48,1536]{1,0:T(8,128)S(1)}, f32[48,1536]{1,0:T(8,128)}, u32[]{:S(2)}) copy-start(f32[48,1536]{1,0:T(8,128)} %param.39) | copy-start | bytes 884740
  1256.6 51.9 %copy-start.35 = (f32[48,1536]{1,0:T(8,128)S(1)}, f32[48,1536]{1,0:T(8,128)}, u32[]{:S(2)}) copy-start(f32[48,1536]{1,0:T(8,128)} %reduce-scatter.20.cloned.1.call-done) | copy-start | bytes 884740
  1256.6 51.9 %copy-start.36 = (f32[48,1536]{1,0:T(8,128)S(1)}, f32[48,1536]{1,0:T(8,128)}, u32[]{:S(2)}) copy-start(f32[48,1536]{1,0:T(8,128)} %reduce-scatter.18.cloned.1.call-done) | copy-start | bytes 884740
  1256.6 51.9 %copy-start.48 = (f32[48,1536]{1,0:T(8,128)S(1)}, f32[48,1536]{1,0:T(8,128)}, u32[]{:S(2)}) copy-start(f32[48,1536]{1,0:T(8,128)} %param.49) | copy-start | bytes 884740
  (77 other events, 578.2 us)
Sparse Core Ops, SparseCore 0:
  10.9 50.2 all-gather.4
  64.0 37.1 all-gather.6
  192.3 97.2 all-reduce.8
  331.7 55.7 all-reduce.10
  390.2 42.2 all-gather.8
  435.1 40.9 all-gather.10
  493.4 93.1 all-reduce.12
  674.8 55.7 all-reduce.14
  785.3 55.7 all-reduce.16
  843.8 28.2 reduce-scatter.9
  876.0 75.5 reduce-scatter.19
  955.8 74.5 reduce-scatter.17
  1034.4 54.6 reduce-scatter.21
  1093.2 61.9 reduce-scatter.15
  1159.1 89.0 reduce-scatter.13
  1251.0 77.9 reduce-scatter.11
where the time goes:
time: 1350 us; the launch traced here: 1340 us
  waiting for transfers between devices  734 us (54%)
  matrix products  247 us (18%)
  local copies, waits for them, and re-layouts  188 us (14%)
  other arithmetic  110 us (8%)
  blocking collectives  41 us (3%)
  between operations  21 us (2%)
    psum x1, waiting for transfers between devices, on_device(): lax.psum(jnp.einsum('rlf,df->rld', slope_pre, up_kernel, preferred_elemen...  93.2 us
    reduce_scatter x1, waiting for transfers between devices, on_device(): lax.psum_scatter(slope_in, 'dp', scatter_dimension=0, tiled=True)  91.4 us
    psum x1, waiting for transfers between devices, on_device(): hidden_one = hidden_zero + lax.psum(self_term, 'tensor')  86.8 us
    reduce_scatter x1, waiting for transfers between devices, on_device(): lax.psum_scatter(slope_up, 'dp', scatter_dimension=0, tiled=True)  77.1 us
    reduce_scatter x1, waiting for transfers between devices, on_device(): lax.psum_scatter(slope_out, 'dp', scatter_dimension=0, tiled=True)  64 us
    unnamed x17, waiting for transfers between devices  56.1 us
    psum x1, waiting for transfers between devices, on_device(): lax.psum(jnp.einsum('rle,de->rld', slope_cross_query, input_kernel_list[:...  54.3 us
    psum x1, waiting for transfers between devices, on_device(): lax.psum(cross_term.astype(jnp.bfloat16), 'tensor').astype(jnp.float32)  53.4 us
  transfers between devices with their start and end apart: 16, of which 13 were waited for; matrix products, arithmetic and copies ran while one was open for 25% of the time, Pallas kernels for 0%

commit v1 on v0

v1 whole, which is shorter than its diff:
```python
import jax
import jax.numpy as jnp
from jax import lax
from jax.experimental import pallas as pl
from jax.experimental.pallas import tpu as pltpu
from jax.sharding import PartitionSpec as P

STEP = 10
NORM_EPS = 1e-06
CLIP_NORM = 1.0
BETA_ONE = 0.9
BETA_TWO = 0.95
ADAM_EPS = 1e-08
MATRIX_RATE = 0.08
SMALL_RATE = 0.8
DECAY_RATE = 0.1
GELU_SCALE = 0.7978845608028654
GELU_CUBIC = 0.044715
MASKED = -1e30
TABLE = 384
NT = (((1,), (1,)), ((), ()))
TN = (((0,), (0,)), ((), ()))


def dot(a, b, dims=(((1,), (0,)), ((), ()))):
    return lax.dot_general(a, b, dims, preferred_element_type=jnp.float32)


def lanes(shape):
    return lax.broadcasted_iota(jnp.int32, shape, len(shape) - 1)


def half_of(values, which):
    return jnp.where((lanes(values.shape) >= 64) == (which == 1), values, jnp.zeros_like(values))


def column(values, index):
    return jnp.sum(jnp.where(lanes(values.shape) == index, values, 0.0), axis=-1, keepdims=True)


def cross_forward_kernel(q_ref, k_ref, v_ref, dec_ref, mem_ref, o_ref, lse_ref):
    pair = pl.program_id(1)
    query, key, value = q_ref[0], k_ref[0], v_ref[0]
    allowed = dec_ref[0] == mem_ref[0]
    mixed, logs = forward_pair(query, key, value, [None, None], allowed)
    o_ref[0] = mixed.astype(o_ref.dtype)
    store_logs(lse_ref, logs, pair)


def store_logs(lse_ref, logs, pair):
    @pl.when(pair == 0)
    def _():
        lse_ref[0] = jnp.zeros(lse_ref.shape[1:], jnp.float32)

    lane = lanes(lse_ref.shape[1:])
    kept = lse_ref[0]
    for which in range(2):
        kept = jnp.where(lane == 2 * pair + which, logs[which], kept)
    lse_ref[0] = kept


def forward_pair(query, key, value, biases, allowed):
    mixed = jnp.zeros(query.shape, jnp.float32)
    logs = []
    for which in range(2):
        scores = dot(half_of(query, which), key, NT)
        if biases[which] is not None:
            scores = scores + biases[which]
        scores = jnp.where(allowed, scores, MASKED)
        top = jnp.max(scores, axis=-1, keepdims=True)
        weights = jnp.exp(scores - top)
        total = jnp.sum(weights, axis=-1, keepdims=True)
        logs.append(top + jnp.log(total))
        mixed = mixed + dot(weights.astype(jnp.bfloat16), half_of(value, which)) * (1.0 / total)
    return mixed, logs


def backward_pair(query, key, value, mixed, upstream, logs, biases, allowed):
    slope_q = jnp.zeros(query.shape, jnp.float32)
    slope_k = jnp.zeros(key.shape, jnp.float32)
    slope_v = jnp.zeros(key.shape, jnp.float32)
    grads = []
    product = upstream.astype(jnp.float32) * mixed.astype(jnp.float32)
    for which in range(2):
        query_half = half_of(query, which)
        up_half = half_of(upstream, which)
        scores = dot(query_half, key, NT)
        if biases[which] is not None:
            scores = scores + biases[which]
        prob = jnp.exp(jnp.where(allowed, scores - logs[which], MASKED))
        slope_p = dot(up_half, value, NT)
        inner = jnp.sum(half_of(product, which), axis=-1, keepdims=True)
        grad = (prob * (slope_p - inner)).astype(jnp.bfloat16)
        slope_q = slope_q + dot(grad, half_of(key, which))
        slope_k = slope_k + dot(grad, query_half, TN)
        slope_v = slope_v + dot(prob.astype(jnp.bfloat16), up_half, TN)
        grads.append(grad)
    return slope_q, slope_k, slope_v, grads


def cross_backward_kernel(
    q_ref, k_ref, v_ref, dec_ref, mem_ref, o_ref, lse_ref, up_ref, dq_ref, dk_ref, dv_ref
):
    pair = pl.program_id(1)
    allowed = dec_ref[0] == mem_ref[0]
    logs = [column(lse_ref[0], 2 * pair + which) for which in range(2)]
    slope_q, slope_k, slope_v, _ = backward_pair(
        q_ref[0], k_ref[0], v_ref[0], o_ref[0], up_ref[0], logs, [None, None], allowed
    )
    dq_ref[0] = slope_q.astype(jnp.bfloat16)
    dk_ref[0] = slope_k.astype(jnp.bfloat16)
    dv_ref[0] = slope_v.astype(jnp.bfloat16)


def pad_keys(values):
    extra = TABLE - values.shape[0]
    return jnp.concatenate([values, jnp.zeros((extra, values.shape[1]), values.dtype)], axis=0)


def self_allowed(dec_ref, decT_ref):
    length = dec_ref.shape[1]
    rows = lax.broadcasted_iota(jnp.int32, (length, TABLE), 0)
    return (dec_ref[0] == decT_ref[0]) & (lanes((length, TABLE)) <= rows)


def toeplitz(table_ref, which, length):
    spread = jnp.broadcast_to(table_ref[0, which : which + 1, :], (length, TABLE))
    return pltpu.roll(spread, 0, 1, stride=1, stride_axis=0)


def self_forward_kernel(q_ref, k_ref, v_ref, dec_ref, decT_ref, table_ref, o_ref, lse_ref):
    pair = pl.program_id(1)
    length = q_ref.shape[1]
    biases = [toeplitz(table_ref, which, length) for which in range(2)]
    mixed, logs = forward_pair(
        q_ref[0], pad_keys(k_ref[0]), pad_keys(v_ref[0]), biases, self_allowed(dec_ref, decT_ref)
    )
    o_ref[0] = mixed.astype(o_ref.dtype)
    store_logs(lse_ref, logs, pair)


def self_backward_kernel(
    q_ref, k_ref, v_ref, dec_ref, decT_ref, table_ref, o_ref, lse_ref, up_ref,
    dq_ref, dk_ref, dv_ref, diag_ref,
):
    pair, row = pl.program_id(0), pl.program_id(1)
    length = q_ref.shape[1]
    biases = [toeplitz(table_ref, which, length) for which in range(2)]
    logs = [column(lse_ref[0], 2 * pair + which) for which in range(2)]
    slope_q, slope_k, slope_v, grads = backward_pair(
        q_ref[0], pad_keys(k_ref[0]), pad_keys(v_ref[0]), o_ref[0], up_ref[0], logs, biases,
        self_allowed(dec_ref, decT_ref),
    )
    dq_ref[0] = slope_q.astype(jnp.bfloat16)
    dk_ref[0] = slope_k[:length].astype(jnp.bfloat16)
    dv_ref[0] = slope_v[:length].astype(jnp.bfloat16)

    @pl.when(row == 0)
    def _():
        diag_ref[...] = jnp.zeros(diag_ref.shape, jnp.float32)

    for which in range(2):
        diag_ref[0, which : which + 1, :] += diagonal_sums(grads[which].astype(jnp.float32))


def diagonal_sums(values):
    groups = jnp.zeros((8, TABLE), jnp.float32)
    for start in range(0, values.shape[0], 8):
        groups = groups + pltpu.roll(values[start : start + 8], (TABLE - start) % TABLE, 1)
    total = groups[0:1]
    for row in range(1, 8):
        total = total + pltpu.roll(groups, TABLE - row, 1)[row : row + 1]
    return total


def params(count):
    return pltpu.CompilerParams(
        dimension_semantics=("arbitrary",) * count, vmem_limit_bytes=48 * 1024 * 1024
    )


def cross_forward(q, kv, dec, mem):
    rows, length, width = q.shape
    keys = kv.shape[1]
    pairs = width // 128
    lanes_q = pl.BlockSpec((1, length, 128), lambda r, p: (r, 0, p))
    lanes_k = pl.BlockSpec((1, keys, 128), lambda r, p: (r, 0, p))
    lanes_v = pl.BlockSpec((1, keys, 128), lambda r, p: (r, 0, p + pairs))
    return pl.pallas_call(
        cross_forward_kernel,
        grid=(rows, width // 128),
        in_specs=[
            lanes_q, lanes_k, lanes_v,
            pl.BlockSpec((1, length, 1), lambda r, p: (r, 0, 0)),
            pl.BlockSpec((1, 1, keys), lambda r, p: (r, 0, 0)),
        ],
        out_specs=[lanes_q, pl.BlockSpec((1, length, 128), lambda r, p: (r, 0, 0))],
        out_shape=[
            jax.ShapeDtypeStruct((rows, length, width), jnp.bfloat16),
            jax.ShapeDtypeStruct((rows, length, 128), jnp.float32),
        ],
        compiler_params=params(2),
        cost_estimate=cost(4 * rows * length * keys * width, 2 * rows * width * (2 * length + 2 * keys), 2 * rows * length * keys * pairs),
        name="cross_forward",
    )(q, kv, kv, dec, mem)


def cross_backward(q, kv, dec, mem, mixed, logs, upstream):
    rows, length, width = q.shape
    keys = kv.shape[1]
    pairs = width // 128
    lanes_q = pl.BlockSpec((1, length, 128), lambda r, p: (r, 0, p))
    lanes_k = pl.BlockSpec((1, keys, 128), lambda r, p: (r, 0, p))
    lanes_v = pl.BlockSpec((1, keys, 128), lambda r, p: (r, 0, p + pairs))
    return pl.pallas_call(
        cross_backward_kernel,
        grid=(rows, width // 128),
        in_specs=[
            lanes_q, lanes_k, lanes_v,
            pl.BlockSpec((1, length, 1), lambda r, p: (r, 0, 0)),
            pl.BlockSpec((1, 1, keys), lambda r, p: (r, 0, 0)),
            lanes_q, pl.BlockSpec((1, length, 128), lambda r, p: (r, 0, 0)), lanes_q,
        ],
        out_specs=[lanes_q, lanes_k, lanes_k],
        out_shape=[
            jax.ShapeDtypeStruct((rows, length, width), jnp.bfloat16),
            jax.ShapeDtypeStruct((rows, keys, width), jnp.bfloat16),
            jax.ShapeDtypeStruct((rows, keys, width), jnp.bfloat16),
        ],
        compiler_params=params(2),
        cost_estimate=cost(10 * rows * length * keys * width, 2 * rows * width * (4 * length + 4 * keys), 2 * rows * length * keys * pairs),
        name="cross_backward",
    )(q, kv, kv, dec, mem, mixed, logs, upstream)


def self_forward(qkv, dec, decT, table):
    rows, length, width = qkv.shape
    width = width // 3
    pairs = width // 128
    spec = pl.BlockSpec((1, length, 128), lambda r, p: (r, 0, p))
    spec_k = pl.BlockSpec((1, length, 128), lambda r, p: (r, 0, p + pairs))
    spec_v = pl.BlockSpec((1, length, 128), lambda r, p: (r, 0, p + 2 * pairs))
    return pl.pallas_call(
        self_forward_kernel,
        grid=(rows, pairs),
        in_specs=[
            spec, spec_k, spec_v,
            pl.BlockSpec((1, length, 1), lambda r, p: (r, 0, 0)),
            pl.BlockSpec((1, 1, TABLE), lambda r, p: (r, 0, 0)),
            pl.BlockSpec((1, 2, TABLE), lambda r, p: (p, 0, 0)),
        ],
        out_specs=[spec, pl.BlockSpec((1, length, 128), lambda r, p: (r, 0, 0))],
        out_shape=[
            jax.ShapeDtypeStruct((rows, length, width), jnp.bfloat16),
            jax.ShapeDtypeStruct((rows, length, 128), jnp.float32),
        ],
        compiler_params=params(2),
        cost_estimate=cost(4 * rows * length * TABLE * width, 8 * rows * width * length, 2 * rows * length * TABLE * pairs),
        name="self_forward",
    )(qkv, qkv, qkv, dec, decT, table)


def self_backward(qkv, dec, decT, table, mixed, logs, upstream):
    rows, length, width = qkv.shape
    width = width // 3
    pairs = width // 128
    spec = pl.BlockSpec((1, length, 128), lambda p, r: (r, 0, p))
    spec_k = pl.BlockSpec((1, length, 128), lambda p, r: (r, 0, p + pairs))
    spec_v = pl.BlockSpec((1, length, 128), lambda p, r: (r, 0, p + 2 * pairs))
    table_spec = pl.BlockSpec((1, 2, TABLE), lambda p, r: (p, 0, 0))
    out = jax.ShapeDtypeStruct((rows, length, width), jnp.bfloat16)
    return pl.pallas_call(
        self_backward_kernel,
        grid=(pairs, rows),
        in_specs=[
            spec, spec_k, spec_v,
            pl.BlockSpec((1, length, 1), lambda p, r: (r, 0, 0)),
            pl.BlockSpec((1, 1, TABLE), lambda p, r: (r, 0, 0)),
            table_spec, spec,
            pl.BlockSpec((1, length, 128), lambda p, r: (r, 0, 0)), spec,
        ],
        out_specs=[spec, spec, spec, table_spec],
        out_shape=[out, out, out, jax.ShapeDtypeStruct((pairs, 2, TABLE), jnp.float32)],
        compiler_params=params(2),
        cost_estimate=cost(10 * rows * length * TABLE * width, 16 * rows * width * length, 2 * rows * length * TABLE * pairs),
        name="self_backward",
    )(qkv, qkv, qkv, dec, decT, table, mixed, logs, upstream)


SLOPE = GELU_SCALE * 3.0 * GELU_CUBIC
ROW_TILE = 16
FF_TILE = 256


def whole(shape):
    return pl.BlockSpec(shape, lambda *_: (0,) * len(shape))


def cost(flops, moved, exps=0):
    return pl.CostEstimate(flops=int(flops), bytes_accessed=int(moved), transcendentals=int(exps))


def row_scale(hidden):
    return lax.rsqrt(jnp.mean(hidden * hidden, axis=-1, keepdims=True) + NORM_EPS)


def row_back(hidden, gain, upstream):
    factor = row_scale(hidden)
    scaled = upstream * hidden
    inner = jnp.mean(scaled * gain, axis=-1, keepdims=True)
    slope = factor * (upstream * gain) - (factor * factor * factor * inner) * hidden
    return slope, jnp.sum(scaled * factor, axis=0, keepdims=True)


def emit(gradient, keep_ref, send_ref, start, upper):
    halves, blocks, rows, _ = keep_ref.shape
    columns = gradient.shape[1] // halves
    for half in range(halves):
        part = gradient[:, half * columns : (half + 1) * columns]
        part = part.reshape(blocks, 2, rows, columns)
        low, high = part[:, 0], part[:, 1]
        keep = jnp.where(upper, high, low).astype(jnp.bfloat16)
        send = jnp.where(upper, low, high).astype(jnp.bfloat16)
        keep_ref[half, :, :, start : start + columns] = keep
        send_ref[half, :, :, start : start + columns] = send


def call(kernel, name, grid, in_specs, out_specs, out_shape, work, scratch=(), scalars=1):
    return pl.pallas_call(
        kernel,
        grid_spec=pltpu.PrefetchScalarGridSpec(
            num_scalar_prefetch=scalars,
            grid=grid,
            in_specs=in_specs,
            out_specs=out_specs,
            scratch_shapes=scratch,
        ),
        out_shape=out_shape,
        compiler_params=pltpu.CompilerParams(
            dimension_semantics=("arbitrary",) * len(grid), vmem_limit_bytes=56 * 1024 * 1024
        ),
        cost_estimate=work,
        name=name,
    )


def shape_of(shape, kind=jnp.bfloat16):
    return jax.ShapeDtypeStruct(shape, kind)


def project_kernel(up_ref, x_ref, gain_ref, w_ref, n_ref, out_ref):
    @pl.when(pl.program_id(0) == 0)
    def _():
        hidden = x_ref[...].astype(jnp.float32)
        n_ref[...] = (hidden * row_scale(hidden) * gain_ref[0:1]).astype(jnp.bfloat16)

    out_ref[...] = dot(n_ref[...], w_ref[...]).astype(jnp.bfloat16)


def project(upper, hidden, gains, kernels):
    tokens, width = hidden.shape
    count = kernels.shape[1] // width
    return call(
        project_kernel, "project", (count,),
        [whole((tokens, width)), whole(gains.shape), pl.BlockSpec((width, width), lambda g, *_: (0, g))],
        [whole((tokens, width)), pl.BlockSpec((tokens, width), lambda g, *_: (0, g))],
        [shape_of((tokens, width)), shape_of((tokens, count * width))],
        cost(2 * tokens * width * width * count, 2 * width * (tokens * (count + 2) + count * width)),
    )(upper, hidden, gains, kernels)


def memory_project_kernel(up_ref, x_ref, w_ref, out_ref):
    out_ref[...] = dot(x_ref[...], w_ref[...]).astype(jnp.bfloat16)


def memory_project(upper, memory, kernels):
    tokens, width = memory.shape
    wide = kernels.shape[1]
    tile = 256
    return call(
        memory_project_kernel, "memory_project", (tokens // tile,),
        [pl.BlockSpec((tile, width), lambda g, *_: (g, 0)), whole(kernels.shape)],
        pl.BlockSpec((tile, wide), lambda g, *_: (g, 0)),
        shape_of((tokens, wide)),
        cost(2 * tokens * width * wide, 2 * (tokens * (width + wide) + width * wide)),
    )(upper, memory, kernels)


def after_self_kernel(up_ref, x_ref, a_ref, gain_ref, wo_ref, wq_ref, h_ref, n_ref, q_ref):
    hidden = x_ref[...].astype(jnp.float32) + dot(a_ref[...], wo_ref[...], NT)
    h_ref[...] = hidden
    normed = (hidden * row_scale(hidden) * gain_ref[1:2]).astype(jnp.bfloat16)
    n_ref[...] = normed
    q_ref[...] = dot(normed, wq_ref[...]).astype(jnp.bfloat16)


def after_self(upper, inputs, mixed, gains, kernel_o, kernel_q):
    tokens, width = inputs.shape
    tile = tokens // 2
    rows = pl.BlockSpec((tile, width), lambda g, *_: (g, 0))
    return call(
        after_self_kernel, "after_self", (2,),
        [rows, rows, whole(gains.shape), whole(kernel_o.shape), whole(kernel_q.shape)],
        [rows, rows, rows],
        [shape_of((tokens, width), jnp.float32), shape_of((tokens, width)), shape_of((tokens, width))],
        cost(4 * tokens * width * width, tokens * width * 12 + 4 * width * width),
    )(upper, inputs, mixed, gains, kernel_o, kernel_q)


def feed_kernel(
    up_ref, h1_ref, a_ref, gy_ref, gain_ref, wo_ref, w_ref,
    y_ref, g_ref, gh_ref, ga_ref, keep_ref, send_ref, gain_out_ref,
    n_ref, nT_ref, gyT_ref, acc_ref,
):
    step = pl.program_id(0)
    tile = FF_TILE
    width = y_ref.shape[1]

    @pl.when(step == 0)
    def _():
        hidden = h1_ref[...] + dot(a_ref[...], wo_ref[...], NT)
        gh_ref[...] = hidden
        y_ref[...] = hidden
        normed = (hidden * row_scale(hidden) * gain_ref[2:3]).astype(jnp.bfloat16)
        n_ref[...] = normed
        nT_ref[...] = normed.T
        gyT_ref[...] = gy_ref[...].T
        acc_ref[...] = jnp.zeros(acc_ref.shape, jnp.float32)

    wi = w_ref[:, 0, :, :tile].reshape(width, tile)
    wf = w_ref[:, 0, :, tile:].reshape(width, tile)
    u = dot(n_ref[...], wi)
    square = u * u
    bent = jnp.tanh(u * (GELU_SCALE + (GELU_SCALE * GELU_CUBIC) * square))
    half = 0.5 + 0.5 * bent
    act = (u * half).astype(jnp.bfloat16)
    slope = half + (0.5 * u) * (1.0 - bent * bent) * (GELU_SCALE + SLOPE * square)
    gu = (dot(gy_ref[...], wf) * slope).astype(jnp.bfloat16)
    y_ref[...] += dot(act, wf, NT)
    acc_ref[...] += dot(gu, wi, NT)
    g_ref[:, 0, :, :tile] = dot(nT_ref[...], gu).reshape(g_ref.shape[0], g_ref.shape[2], tile).astype(jnp.bfloat16)
    g_ref[:, 0, :, tile:] = dot(gyT_ref[...], act).reshape(g_ref.shape[0], g_ref.shape[2], tile).astype(jnp.bfloat16)

    @pl.when(step == pl.num_programs(0) - 1)
    def _():
        back, gain = row_back(gh_ref[...], gain_ref[2:3], acc_ref[...])
        gain_out_ref[...] = gain
        total = gy_ref[...].astype(jnp.float32) + back
        gh_ref[...] = total
        low = total.astype(jnp.bfloat16)
        ga_ref[...] = dot(low, wo_ref[...]).astype(jnp.bfloat16)
        emit(dot(low.T, a_ref[...]), keep_ref, send_ref, 0, up_ref[0] == 1)


def feed_forward(upper, hidden, mixed, cotangent, gains, kernel_o, weights, split):
    tokens, width = hidden.shape
    blocks, halves, rows, wide = weights.shape
    steps = wide // (2 * FF_TILE)
    spec = pl.BlockSpec((blocks, 1, rows, 2 * FF_TILE), lambda g, *_: (0, g // steps, 0, g % steps))
    full = whole((tokens, width))
    f32 = shape_of((tokens, width), jnp.float32)
    columns = width // halves
    return call(
        feed_kernel, "feed_forward", (halves * steps,),
        [full, full, full, whole(gains.shape), whole(kernel_o.shape), spec],
        [full, spec, full, full, whole(split + (columns,)), whole(split + (columns,)), whole((1, width))],
        [f32, shape_of(weights.shape), f32, shape_of((tokens, width)),
         shape_of(split + (columns,)), shape_of(split + (columns,)), shape_of((1, width), jnp.float32)],
        cost(6 * tokens * width * halves * wide, 40 * tokens * width, tokens * halves * wide / 2),
        scratch=[
            pltpu.VMEM((tokens, width), jnp.bfloat16), pltpu.VMEM((width, tokens), jnp.bfloat16),
            pltpu.VMEM((width, tokens), jnp.bfloat16), pltpu.VMEM((tokens, width), jnp.float32),
        ],
    )(upper, hidden, mixed, cotangent, gains, kernel_o, weights)


def after_cross_kernel(
    up_ref, gq_ref, n_ref, h_ref, gh_ref, a_ref, gain_ref, wq_ref, wo_ref,
    gh1_ref, ga_ref, keep_ref, send_ref, gain_out_ref,
):
    upper = up_ref[0] == 1
    columns = keep_ref.shape[3] // 2
    back, gain = row_back(h_ref[...], gain_ref[1:2], dot(gq_ref[...], wq_ref[...], NT))
    gain_out_ref[...] = gain
    total = gh_ref[...] + back
    gh1_ref[...] = total
    low = total.astype(jnp.bfloat16)
    ga_ref[...] = dot(low, wo_ref[...]).astype(jnp.bfloat16)
    emit(dot(n_ref[...].T, gq_ref[...]), keep_ref, send_ref, 0, upper)
    emit(dot(low.T, a_ref[...]), keep_ref, send_ref, columns, upper)


def after_cross(upper, slope_q, normed, hidden, slope_hidden, mixed, gains, kernel_q, kernel_o, split):
    tokens, width = hidden.shape
    full, square = whole((tokens, width)), whole((width, width))
    piece = split + (2 * (width // split[0]),)
    return call(
        after_cross_kernel, "after_cross", (1,),
        [full, full, full, full, full, whole(gains.shape), square, square],
        [full, full, whole(piece), whole(piece), whole((1, width))],
        [shape_of((tokens, width), jnp.float32), shape_of((tokens, width)),
         shape_of(piece), shape_of(piece), shape_of((1, width), jnp.float32)],
        cost(8 * tokens * width * width, tokens * width * 24 + 8 * width * width),
    )(upper, slope_q, normed, hidden, slope_hidden, mixed, gains, kernel_q, kernel_o)


def outer_kernel(up_ref, x_ref, *refs):
    slopes, keep_ref, send_ref = refs[:-2], refs[-2], refs[-1]
    upper = up_ref[0] == 1
    columns = keep_ref.shape[3] // len(slopes)
    across = x_ref[...].T
    for place, slope in enumerate(slopes):
        emit(dot(across, slope[...]), keep_ref, send_ref, place * columns, upper)


def outer(upper, rows, slopes, split, name):
    tokens, width = rows.shape
    piece = split + (len(slopes) * (width // split[0]),)
    return call(
        outer_kernel, name, (1,),
        [whole(rows.shape)] + [whole(slope.shape) for slope in slopes],
        [whole(piece), whole(piece)],
        [shape_of(piece), shape_of(piece)],
        cost(2 * tokens * width * width * len(slopes), 2 * width * (tokens + width) * (1 + len(slopes))),
    )(upper, rows, *slopes)


def memory_back_kernel(up_ref, gk_ref, gv_ref, w_ref, out_ref):
    width = gk_ref.shape[1]
    out_ref[...] = dot(gk_ref[...], w_ref[:, :width], NT) + dot(gv_ref[...], w_ref[:, width:], NT)


def memory_back(upper, slope_k, slope_v, kernels):
    tokens, width = slope_k.shape
    tile = 256
    rows = pl.BlockSpec((tile, width), lambda g, *_: (g, 0))
    return call(
        memory_back_kernel, "memory_back", (tokens // tile,),
        [rows, rows, whole(kernels.shape)], rows, shape_of((tokens, width), jnp.float32),
        cost(4 * tokens * width * width, 8 * tokens * width + 4 * width * width),
    )(upper, slope_k, slope_v, kernels)


def input_back_kernel(up_ref, gq_ref, gk_ref, gv_ref, x_ref, gh_ref, gain_ref, w_ref, out_ref, gain_out_ref):
    width = x_ref.shape[1]
    upstream = dot(gq_ref[...], w_ref[:, :width], NT)
    upstream += dot(gk_ref[...], w_ref[:, width : 2 * width], NT)
    upstream += dot(gv_ref[...], w_ref[:, 2 * width :], NT)
    back, gain = row_back(x_ref[...].astype(jnp.float32), gain_ref[0:1], upstream)
    out_ref[...] = (gh_ref[...] + back).astype(jnp.bfloat16)
    gain_out_ref[...] = gain


def input_back(upper, slopes, inputs, slope_hidden, gains, kernels):
    tokens, width = inputs.shape
    full = whole((tokens, width))
    return call(
        input_back_kernel, "input_back", (1,),
        [full] * 5 + [whole(gains.shape), whole(kernels.shape)],
        [full, whole((1, width))],
        [shape_of((tokens, width)), shape_of((1, width), jnp.float32)],
        cost(6 * tokens * width * width, 14 * tokens * width + 6 * width * width),
    )(upper, *slopes, inputs, slope_hidden, gains, kernels)


def assemble_kernel(layout, up_ref, *refs):
    pieces, outs = refs[: len(refs) - len(layout)], refs[len(refs) - len(layout) :]
    upper = up_ref[0] == 1
    for out, group in zip(outs, layout):
        rows = out.shape[0] // 2
        for place, (source, start, columns) in enumerate(group):
            for half in range(2):
                own = pieces[2 * source][half, 0, :, start : start + columns]
                other = pieces[2 * source + 1][half, 0, :, start : start + columns]
                at = (2 * place + half) * columns
                out[:rows, at : at + columns] = jnp.where(upper, other, own)
                out[rows:, at : at + columns] = jnp.where(upper, own, other)


def assemble(upper, pairs, layout):
    _, blocks, rows, _ = pairs[0][0].shape
    pieces = [piece for pair in pairs for piece in pair]
    wides = [sum(2 * columns for _, _, columns in group) for group in layout]
    if rows % ROW_TILE:
        return [
            jnp.concatenate([assemble_plain(upper, pairs[s], b, b + n) for s, b, n in group], axis=1)
            for group in layout
        ]
    spec = lambda piece: pl.BlockSpec((2, 1) + piece.shape[2:], lambda g, *_: (0, g, 0, 0))
    return call(
        lambda *refs: assemble_kernel(layout, *refs), "assemble", (blocks,),
        [spec(piece) for piece in pieces],
        [pl.BlockSpec((2 * rows, wide), lambda g, *_: (g, 0)) for wide in wides],
        [shape_of((2 * rows * blocks, wide)) for wide in wides],
        cost(0, sum(4 * piece.size for piece in pieces)),
    )(upper, *pieces)


def assemble_plain(upper, pair, start, stop):
    own, other = pair
    both = in_order(own[..., start:stop], other[..., start:stop], upper[0] == 1, 2)
    halves, blocks, _, rows, columns = both.shape
    return jnp.transpose(both, (1, 2, 3, 0, 4)).reshape(blocks * 2 * rows, halves * columns)


def axis_bits(size):
    return size.bit_length() - 1


def swap_dp(values, bit):
    count = lax.axis_size("dp")
    return lax.ppermute(values, "dp", [(i, i ^ (1 << bit)) for i in range(count)])


def swap_tensor(values):
    return lax.ppermute(values, "tensor", [(0, 1), (1, 0)])


def bit_set(index, bit):
    return lax.rem(lax.shift_right_logical(index, bit), 2) == 1


def in_order(own, other, upper, axis):
    return jnp.where(
        upper, jnp.stack([other, own], axis=axis), jnp.stack([own, other], axis=axis)
    )


def gather_bit(values, bit, index):
    both = in_order(values, swap_dp(values, bit), bit_set(index, bit), 2)
    return both.reshape((values.shape[0], 2 * values.shape[1]) + values.shape[2:])


def gather_tensor(values):
    return jnp.concatenate([values, swap_tensor(values)], axis=0)


def gather_rows(shard, index):
    bits = axis_bits(lax.axis_size("dp"))
    values = shard[None, None]
    for bit in range(bits - 1, 1, -1):
        values = gather_bit(values, bit, index)
    cut = values.shape[-1] // 2
    first = gather_tensor(gather_bit(values[..., :cut], 1, index))
    second = gather_bit(gather_tensor(values[..., cut:]), 1, index)
    return [(part, swap_dp(part, 0)) for part in (first, second)]


def pick(values, upper, axis):
    return jnp.where(
        upper,
        lax.index_in_dim(values, 1, axis, keepdims=False),
        lax.index_in_dim(values, 0, axis, keepdims=False),
    )


def add_low(left, right):
    return left.astype(jnp.float32) + right.astype(jnp.float32)


def reduce_bit(values, bit, index):
    shape = values.shape
    values = values.astype(jnp.bfloat16).reshape((shape[0], shape[1] // 2, 2) + shape[2:])
    upper = bit_set(index, bit)
    return add_low(pick(values, upper, 2), swap_dp(pick(values, ~upper, 2), bit))


def reduce_tensor(values):
    values = values.astype(jnp.bfloat16)
    return add_low(values[0:1], swap_tensor(values[1:2]))


def scatter_group(pieces, cut, index):
    bits = axis_bits(lax.axis_size("dp"))
    values = jnp.concatenate(
        [add_low(kept, swap_dp(sent, 0)) for kept, sent in pieces], axis=-1
    ).astype(jnp.bfloat16)
    first = reduce_bit(reduce_tensor(values[..., :cut]), 1, index)
    second = reduce_tensor(reduce_bit(values[..., cut:], 1, index))
    values = jnp.concatenate([first, second], axis=-1)
    for bit in range(2, bits):
        values = reduce_bit(values, bit, index)
    return values[0, 0]


def sum_everywhere(values):
    values = values + swap_tensor(values)
    for bit in range(axis_bits(lax.axis_size("dp"))):
        values = values + swap_dp(values, bit)
    return values


def reverse_distance(table):
    return jnp.roll(table[:, ::-1], 1, axis=1)


def adam_update(weight, gradient, moment, square, learn_rate, weight_decay):
    new_moment = BETA_ONE * moment + (1.0 - BETA_ONE) * gradient
    new_square = BETA_TWO * square + (1.0 - BETA_TWO) * gradient * gradient
    direction = (
        new_moment
        / (1.0 - BETA_ONE**STEP)
        / (jnp.sqrt(new_square / (1.0 - BETA_TWO**STEP)) + ADAM_EPS)
    )
    return (new_moment, new_square, weight - learn_rate * (direction + weight_decay * weight))


def interleave(left, right):
    rows = left.shape[0]
    parts = [part.reshape(rows, -1, 1, FF_TILE) for part in (left, right)]
    return jnp.concatenate(parts, axis=2).reshape(rows, -1)


def take_apart(values):
    parts = values.reshape(values.shape[0], -1, 2, FF_TILE)
    return (
        parts[:, :, 0].reshape(values.shape[0], -1),
        parts[:, :, 1].reshape(values.shape[0], -1),
    )


def on_device(
    inputs,
    memory,
    dec_segments,
    mem_segments,
    mem_lengths,
    buckets,
    cotangent,
    attention_in,
    attention_out,
    expand_weight,
    contract_weight,
    norm_gains,
    position_bias,
    moment_attention_in,
    square_attention_in,
    moment_attention_out,
    square_attention_out,
    moment_expand,
    square_expand,
    moment_contract,
    square_contract,
    moment_gains,
    square_gains,
    moment_bias,
    square_bias,
):
    low = jnp.bfloat16
    everywhere = ("dp", "tensor")
    tensor_count = lax.axis_size("tensor")
    tensor_index = lax.axis_index("tensor")
    index = lax.axis_index("dp")
    rows = inputs.shape[0] // tensor_count
    length, width = inputs.shape[1], inputs.shape[2]
    keys = memory.shape[1]
    shard_rows = attention_in.shape[0]
    shards = width // shard_rows
    columns = attention_in.shape[2]
    aligned = shard_rows % ROW_TILE == 0
    upper = bit_set(index, 0).astype(jnp.int32)[None]
    split = (tensor_count, shards // 2, shard_rows)

    def own_rows(values):
        return lax.dynamic_slice_in_dim(values, tensor_index * rows, rows, 0)

    def flat(values):
        return values.reshape(values.shape[0] * values.shape[1], values.shape[2])

    def in_rows(values, size):
        return values.reshape(rows, size, values.shape[-1])

    wa = attention_in.astype(low)
    wo = attention_out.astype(low)
    piece_self = gather_rows(
        jnp.concatenate([wa[:, 0], wa[:, 1], wa[:, 2], wo[:, 0]], axis=1), index
    )
    piece_cross = gather_rows(
        jnp.concatenate([wa[:, 4], wa[:, 5], wa[:, 3], wo[:, 1]], axis=1), index
    )
    feed_shard = interleave(expand_weight.astype(low), contract_weight.astype(low))
    feed_weights = lax.all_gather(feed_shard, everywhere, axis=0, tiled=True).reshape(
        shards, tensor_count, shard_rows, feed_shard.shape[1]
    )
    if not aligned:
        feed_weights = jnp.transpose(feed_weights, (1, 0, 2, 3)).reshape(
            1, tensor_count, width, feed_shard.shape[1]
        )
    kernel_qkv, kernel_so = assemble(
        upper, piece_self, [[(0, 0, columns), (0, columns, columns), (1, 0, columns)], [(1, columns, columns)]]
    )
    kernel_ckv, kernel_cq, kernel_co = assemble(
        upper, piece_cross, [[(0, 0, columns), (0, columns, columns)], [(1, 0, columns)], [(1, columns, columns)]]
    )

    decoder_ids = own_rows(dec_segments)
    key_index = jnp.arange(keys, dtype=jnp.int32)
    memory_ids = jnp.where(
        key_index[None, :] < own_rows(mem_lengths)[:, None], own_rows(mem_segments), -1
    )
    dec = decoder_ids[:, :, None]
    dec_across = jnp.pad(decoder_ids, ((0, 0), (0, TABLE - length)), constant_values=-1)[:, None]
    mem_across = memory_ids[:, None]
    own_heads = position_bias.shape[1]
    heads = own_heads * tensor_count
    both_bias = jnp.concatenate([position_bias, swap_tensor(position_bias)], axis=1)
    lookup = (
        buckets[None, :] == jnp.arange(position_bias.shape[0], dtype=jnp.int32)[:, None]
    ).astype(jnp.float32)
    lookup = jnp.pad(lookup, ((0, 0), (0, TABLE - length)))
    table = jnp.einsum(
        "gd,gm->md", lookup, both_bias, precision=lax.Precision.HIGHEST,
        preferred_element_type=jnp.float32,
    )
    table = reverse_distance(table).reshape(heads // 2, 2, TABLE)
    gains = norm_gains.T

    own_inputs = flat(own_rows(inputs))
    own_memory = flat(own_rows(memory))
    own_cotangent = flat(own_rows(cotangent))
    normed_zero, qkv = project(upper, own_inputs, gains, kernel_qkv)
    qkv = in_rows(qkv, length)
    cross_kv = in_rows(memory_project(upper, own_memory, kernel_ckv), keys)
    self_mixed, self_logs = self_forward(qkv, dec, dec_across, table)
    hidden_one, normed_one, cross_query = after_self(
        upper, own_inputs, flat(self_mixed), gains, kernel_so, kernel_cq
    )
    cross_query = in_rows(cross_query, length)
    cross_mixed, cross_logs = cross_forward(cross_query, cross_kv, dec, mem_across)
    split_or_whole = split if aligned else (tensor_count, 1, width // 2)
    output, feed_slopes, slope_two, slope_cm, keep_co, send_co, gain_two = feed_forward(
        upper, hidden_one, flat(cross_mixed), own_cotangent, gains, kernel_co, feed_weights, split_or_whole
    )
    output = in_rows(output, length)

    def halves_of(kept, sent):
        if aligned:
            return kept, sent
        low_half = jnp.where(upper[0] == 1, sent, kept)
        high_half = jnp.where(upper[0] == 1, kept, sent)
        both = jnp.concatenate([low_half, high_half], axis=2)
        both = both.reshape((tensor_count, shards // 2, 2, shard_rows, both.shape[-1]))
        return pick(both, upper[0] == 1, 2), pick(both, upper[0] == 0, 2)

    if not aligned:
        feed_slopes = jnp.transpose(
            feed_slopes.reshape(tensor_count, shards, shard_rows, feed_slopes.shape[-1]), (1, 0, 2, 3)
        )
    share_feed = lax.psum_scatter(
        feed_slopes.reshape(-1, feed_slopes.shape[-1]), everywhere, scatter_dimension=0, tiled=True
    ).astype(jnp.float32)

    slope_cq, slope_ck, slope_cv = cross_backward(
        cross_query, cross_kv, dec, mem_across, cross_mixed, cross_logs, in_rows(slope_cm, length)
    )
    slope_one, slope_sm, keep_qo, send_qo, gain_one = after_cross(
        upper, flat(slope_cq), normed_one, hidden_one, slope_two, flat(self_mixed), gains,
        kernel_cq, kernel_so, split_or_whole,
    )
    keep_kv, send_kv = outer(
        upper, own_memory, [flat(slope_ck), flat(slope_cv)], split_or_whole, "memory_outer"
    )
    share_cross = scatter_group(
        [halves_of(keep_co, send_co), halves_of(keep_qo, send_qo), halves_of(keep_kv, send_kv)],
        1024, index,
    )
    slope_q, slope_k, slope_v, diagonals = self_backward(
        qkv, dec, dec_across, table, self_mixed, self_logs, in_rows(slope_sm, length)
    )
    slopes_self = [flat(slope_q), flat(slope_k), flat(slope_v)]
    share_self = scatter_group(
        [halves_of(*outer(upper, normed_zero, slopes_self, split_or_whole, "self_outer"))], 512, index
    )
    memory_grad = in_rows(
        memory_back(upper, flat(slope_ck), flat(slope_cv), kernel_ckv), keys
    )
    input_slope, gain_zero = input_back(
        upper, slopes_self, own_inputs, slope_one, gains, kernel_qkv
    )
    input_slope = in_rows(input_slope, length)
    input_grad = (
        in_order(input_slope, swap_tensor(input_slope), tensor_index == 1, 0)
        .reshape(inputs.shape)
        .astype(jnp.float32)
    )

    bias_local = jnp.einsum(
        "gd,md->gm", lookup, reverse_distance(diagonals.reshape(heads, TABLE)),
        precision=lax.Precision.HIGHEST, preferred_element_type=jnp.float32,
    )
    bias_local = jnp.where(
        tensor_index == 1, jnp.roll(bias_local, own_heads, axis=1), bias_local
    )
    small = jnp.concatenate([gain_zero[0], gain_one[0], gain_two[0], bias_local.reshape(-1)])
    small = sum_everywhere(small)
    gain_sums = small[: 3 * width].reshape(3, width)
    bias_sums = small[3 * width :].reshape(bias_local.shape)
    square_sum = sum_everywhere(
        sum(jnp.sum(share * share) for share in (share_self, share_cross, share_feed))
    )
    grad_norm = jnp.sqrt(square_sum + jnp.sum(small * small))
    clip_factor = jnp.minimum(1.0, CLIP_NORM / (grad_norm + 1e-06))

    parts_self = [share_self[:, i * columns : (i + 1) * columns] for i in range(3)]
    parts_cross = [share_cross[:, i * columns : (i + 1) * columns] for i in range(5)]
    slope_in = jnp.stack(parts_self + [parts_cross[1], parts_cross[3], parts_cross[4]], axis=1)
    slope_out = jnp.stack([parts_cross[2], parts_cross[0]], axis=1)
    slope_up, slope_down = take_apart(share_feed)
    shared_gains = lax.dynamic_slice_in_dim(gain_sums, index * shard_rows, shard_rows, 1).T
    old_gains = lax.dynamic_slice_in_dim(norm_gains, index * shard_rows, shard_rows, 0)
    bias_share = lax.dynamic_slice_in_dim(bias_sums, tensor_index * own_heads, own_heads, 1)
    new_in = adam_update(
        attention_in, slope_in * clip_factor, moment_attention_in, square_attention_in,
        MATRIX_RATE, DECAY_RATE,
    )
    new_out = adam_update(
        attention_out, slope_out * clip_factor, moment_attention_out, square_attention_out,
        MATRIX_RATE, DECAY_RATE,
    )
    new_up = adam_update(
        expand_weight, slope_up * clip_factor, moment_expand, square_expand,
        MATRIX_RATE, DECAY_RATE,
    )
    new_down = adam_update(
        contract_weight, slope_down * clip_factor, moment_contract, square_contract,
        MATRIX_RATE, DECAY_RATE,
    )
    new_gains = adam_update(
        old_gains, shared_gains * clip_factor, moment_gains, square_gains, SMALL_RATE, 0.0
    )
    new_bias = adam_update(
        position_bias, bias_share * clip_factor, moment_bias, square_bias, SMALL_RATE, 0.0
    )
    return (
        (output, input_grad, memory_grad, grad_norm)
        + new_in + new_out + new_up + new_down + new_gains + new_bias
    )


def solution(mesh):
    return jax.shard_map(
        on_device,
        mesh=mesh,
        in_specs=(
            P("dp", None, None),
            P("dp", None, None),
            P("dp", None),
            P("dp", None),
            P("dp"),
            P(),
            P("dp", None, None),
            P("dp", None, "tensor"),
            P("dp", None, "tensor"),
            P("dp", "tensor"),
            P("dp", "tensor"),
            P(),
            P(None, "tensor"),
            P("dp", None, "tensor"),
            P("dp", None, "tensor"),
            P("dp", None, "tensor"),
            P("dp", None, "tensor"),
            P("dp", "tensor"),
            P("dp", "tensor"),
            P("dp", "tensor"),
            P("dp", "tensor"),
            P("dp", None),
            P("dp", None),
            P(None, "tensor"),
            P(None, "tensor"),
        ),
        out_specs=(
            P(("dp", "tensor"), None, None),
            P("dp", None, None),
            P(("dp", "tensor"), None, None),
            P(),
            P("dp", None, "tensor"),
            P("dp", None, "tensor"),
            P("dp", None, "tensor"),
            P("dp", None, "tensor"),
            P("dp", None, "tensor"),
            P("dp", None, "tensor"),
            P("dp", "tensor"),
            P("dp", "tensor"),
            P("dp", "tensor"),
            P("dp", "tensor"),
            P("dp", "tensor"),
            P("dp", "tensor"),
            P("dp", None),
            P("dp", None),
            P("dp", None),
            P(None, "tensor"),
            P(None, "tensor"),
            P(None, "tensor"),
        ),
        check_vma=False,
    )
```

time: 1350 us -> 473 us (0.35)
  waiting for transfers between devices: 734 us -> 125 us
  matrix products: 247 us -> 1.04 us
  Pallas kernels: 0 us -> 202 us
  local copies, waits for them, and re-layouts: 188 us -> 33.1 us
  other arithmetic: 110 us -> 36.1 us
  starting transfers between devices: 0.84 us -> 48.4 us
  blocking collectives: 41 us -> 0 us
    psum x5 -> x0, waiting for transfers between devices: 309 us -> none  [the longest x1 93.2 us: on_device(): lax.psum(jnp.einsum('rlf,df->rld', slope_pre, up_kernel, preferred_elemen...]
    reduce_scatter x6 -> x1, waiting for transfers between devices: 293 us -> 0.02 us  [on_device(): lax.psum_scatter(feed_slopes.reshape(-1, feed_slopes.shape[-1]), everywhe...]
    dot_general x43 -> x2, matrix products: 247 us -> 1.04 us  [the longest x1 0.82 us: on_device(): jnp.einsum('gd,gm->md', lookup, both_bias, precision=lax.Precision.HIGHES...]
    pallas_call x0 -> x15, Pallas kernels: none -> 202 us  [the longest x1 33.5 us: feed_forward(): call(feed_kernel, 'feed_forward', (halves * steps,), [full, full, full, w...]
    ppermute x0 -> x44, waiting for transfers between devices: none -> 125 us  [the longest x32 98.5 us: swap_dp(): return lax.ppermute(values, 'dp', [(i, i ^ 1 << bit) for i in range(count)])]
    all_gather x4 -> x1, waiting for transfers between devices: 75.3 us -> 0.01 us  [on_device(): lax.all_gather(feed_shard, everywhere, axis=0, tiled=True)]
    reshape x5 -> x8, local copies, waits for them, and re-layouts: 76.1 us -> 3.66 us  [the longest x1 1.54 us: take_apart(): parts = values.reshape(values.shape[0], -1, 2, FF_TILE)]
    unnamed x17 -> x2, waiting for transfers between devices: 56.1 us -> 0.03 us
  transfers between devices with their start and end apart: 16 -> 46, of which waited for: 13 -> 24; matrix products, arithmetic and copies ran while one was open for 25% -> 9% of each run, Pallas kernels for 0% -> 36%
where the time goes in v1:
time: 473 us; the launch traced here: 467 us
  Pallas kernels  202 us (43%)
  waiting for transfers between devices  125 us (26%)
  starting transfers between devices  48.4 us (10%)
  other arithmetic  36.1 us (8%)
  local copies, waits for them, and re-layouts  33.1 us (7%)
  between operations  21.9 us (5%)
    ppermute x32, waiting for transfers between devices, swap_dp(): return lax.ppermute(values, 'dp', [(i, i ^ 1 << bit) for i in range(count)])  98.5 us
    pallas_call x1, Pallas kernels, feed_forward(): call(feed_kernel, 'feed_forward', (halves * steps,), [full, full, full, w...  33.5 us
    ppermute x32, starting transfers between devices, swap_dp(): return lax.ppermute(values, 'dp', [(i, i ^ 1 << bit) for i in range(count)])  31 us
    pallas_call x1, Pallas kernels, cross_backward(): pl.pallas_call(cross_backward_kernel, grid=(rows, width // 128), in_specs...  29.2 us
    ppermute x12, waiting for transfers between devices, swap_tensor(): return lax.ppermute(values, 'tensor', [(0, 1), (1, 0)])  26.5 us
    pallas_call x1, Pallas kernels, self_backward(): pl.pallas_call(self_backward_kernel, grid=(pairs, rows), in_specs=[spec,...  23.6 us
    pallas_call x1, Pallas kernels, cross_forward(): pl.pallas_call(cross_forward_kernel, grid=(rows, width // 128), in_specs=...  19.3 us
    unnamed x120, local copies, waits for them, and re-layouts  19.2 us
  transfers between devices with their start and end apart: 46, of which 24 were waited for; matrix products, arithmetic and copies ran while one was open for 9% of the time, Pallas kernels for 36%

profile of v1, /device:TPU:0, one launch (start us, length us, event | category | flops | bytes accessed | tf_op | source)
XLA Modules:
  0.0 467.3 jit_solution(11736192874501100793)
XLA Ops:
  11.3 4.1 collective-permute-start.9
  15.5 11.0 %collective-permute-done.9 = bf16[1,1,48,1536]{3,2,1,0:T(8,128)(2,1)S(1)} collective-permute-done((bf16[1,1,48,1536]{3,2,1,0:T(8,128)(2,1)S(1)}, bf16[1,1,48,1536]{3,2,1,0:T(8,128)(2,1)S(1)}, u32[]{:S(2)}, u32[]{:S(2)}) %collective-permute-start.9) | collective-permute-done | bytes 147488 | tf_op jit(solution)/shard_map/ppermute | solution.py:612
  28.6 3.9 collective-permute-done
  33.8 7.6 %collective-permute-done.10 = bf16[1,2,48,1536]{3,2,1,0:T(8,128)(2,1)S(1)} collective-permute-done((bf16[1,2,48,1536]{3,2,1,0:T(8,128)(2,1)S(1)}, bf16[1,2,48,1536]{3,2,1,0:T(8,128)(2,1)S(1)}, u32[]{:S(2)}, u32[]{:S(2)}) %collective-permute-start.10) | collective-permute-done | bytes 294944 | tf_op jit(solution)/shard_map/ppermute | solution.py:612
  44.9 4.3 collective-permute-done.1
  51.9 4.7 collective-permute-done.14
  62.9 3.5 collective-permute-done.5
  69.9 13.5 %collective-permute-done.2 = bf16[1,4,48,768]{3,2,1,0:T(8,128)(2,1)} collective-permute-done((bf16[1,4,48,768]{3,2,1,0:T(8,128)(2,1)}, bf16[1,4,48,768]{3,2,1,0:T(8,128)(2,1)}, u32[]{:S(2)}, u32[]{:S(2)}) %collective-permute-start.2) | collective-permute-done | bytes 294944 | tf_op jit(solution)/shard_map/ppermute | solution.py:612
  93.5 9.9 %collective-permute-done.6 = bf16[2,4,48,768]{3,2,1,0:T(8,128)(2,1)} collective-permute-done((bf16[2,4,48,768]{3,2,1,0:T(8,128)(2,1)}, bf16[2,4,48,768]{3,2,1,0:T(8,128)(2,1)}, u32[]{:S(2)}, u32[]{:S(2)}) %collective-permute-start.6) | collective-permute-done | bytes 589856 | tf_op jit(solution)/shard_map/ppermute | solution.py:612
  116.5 7.0 %assemble.3 = (bf16[768,1536]{1,0:T(8,128)(2,1)}, bf16[768,768]{1,0:T(8,128)(2,1)}, bf16[768,768]{1,0:T(8,128)(2,1)}) custom-call(s32[1]{0:T(128)} %bitcast.refs_0_.up_ref, bf16[2,8,48,768]{3,2,1,0:T(8,128)(2,1)} %pad_maximum_fusion.2.refs_1_, bf16[2,8,48,768]{3,2,1,0:T(8,128)(2,1)} %collective-permute-done.13.refs_2_, bf16[2,8,48,768]{3,2,1,0:T(8,128)(2,1)} %bitcast.284, ...), custom_call_target="tpu_custom_call" | custom-call | bytes 9437184 | tf_op jit(solution)/shard_map/assemble/pallas_call | solution.py:590
  123.6 7.0 %assemble.2 = (bf16[768,2304]{1,0:T(8,128)(2,1)}, bf16[768,768]{1,0:T(8,128)(2,1)}) custom-call(s32[1]{0:T(128)} %bitcast.refs_0_.up_ref, bf16[2,8,48,768]{3,2,1,0:T(8,128)(2,1)} %pad_maximum_fusion.1.refs_1_, bf16[2,8,48,768]{3,2,1,0:T(8,128)(2,1)} %collective-permute-done.4.refs_2_, bf16[2,8,48,768]{3,2,1,0:T(8,128)(2,1)} %bitcast.18.refs_3_, ...), custom_call_target="tpu_custom_call" | custom-call | bytes 9437184 | tf_op jit(solution)/shard_map/assemble/pallas_call | solution.py:590
  130.5 6.2 %project.1 = (bf16[576,768]{1,0:T(8,128)(2,1)}, bf16[576,2304]{1,0:T(8,128)(2,1)}) custom-call(s32[1]{0:T(128)} %bitcast.refs_0_.up_ref, bf16[576,768]{1,0:T(8,128)(2,1)} %bitcast.285, f32[3,768]{1,0:T(4,128)} %bitcast.319, bf16[768,2304]{1,0:T(8,128)(2,1)} %get-tuple-element.61.w_ref), custom_call_target="tpu_custom_call" | custom-call | flops 2038431744 | bytes 7962624 | tf_op jit(solution)/shard_map/project/pallas_call | solution.py:363
  138.4 14.1 %self_forward.1 = (bf16[2,288,768]{2,1,0:T(8,128)(2,1)S(1)}, f32[2,288,128]{2,1,0:T(8,128)S(1)}) custom-call(bf16[2,288,2304]{2,1,0:T(8,128)(2,1)S(1)} %bitcast.255, bf16[2,288,2304]{2,1,0:T(8,128)(2,1)S(1)} %bitcast.256, bf16[2,288,2304]{2,1,0:T(8,128)(2,1)S(1)} %bitcast.257, s32[2,288,1]{2,1,0:T(8,128)S(1)} %copy.156.dec_ref, ...), custom_call_target="tpu_custom_call" | custom-call | flops 679477248 | bytes 3538944 | tf_op jit(solution)/shard_map/self_forward/pallas_call | solution.py:243
  153.5 5.3 %after_self.1 = (f32[576,768]{1,0:T(8,128)}, bf16[576,768]{1,0:T(8,128)(2,1)}, bf16[576,768]{1,0:T(8,128)(2,1)}) custom-call(s32[1]{0:T(128)} %bitcast.refs_0_.up_ref, bf16[576,768]{1,0:T(8,128)(2,1)} %bitcast.286, bf16[576,768]{1,0:T(8,128)(2,1)} %bitcast.264, f32[3,768]{1,0:T(4,128)} %bitcast.320, bf16[768,768]{1,0:T(8,128)(2,1)} %get-tuple-element.64.wo_ref, ...), custom_call_target="tpu_custom_call" | custom-call | flops 1358954496 | bytes 7667712 | tf_op jit(solution)/shard_map/after_self/pallas_call | solution.py:401
  158.8 10.6 %memory_project.1 = bf16[2048,1536]{1,0:T(8,128)(2,1)} custom-call(s32[1]{0:T(128)} %bitcast.refs_0_.up_ref, bf16[2048,768]{1,0:T(8,128)(2,1)} %bitcast.292, bf16[768,1536]{1,0:T(8,128)(2,1)} %get-tuple-element.68.w_ref), custom_call_target="tpu_custom_call" | custom-call | flops 4831838208 | bytes 11796480 | tf_op jit(solution)/shard_map/memory_project/pallas_call | solution.py:380
  169.4 19.3 %cross_forward.1 = (bf16[2,288,768]{2,1,0:T(8,128)(2,1)S(1)}, f32[2,288,128]{2,1,0:T(8,128)S(1)}) custom-call(bf16[2,288,768]{2,1,0:T(8,128)(2,1)S(1)} %bitcast.266, bf16[2,1024,1536]{2,1,0:T(8,128)(2,1)} %bitcast.272, bf16[2,1024,1536]{2,1,0:T(8,128)(2,1)} %bitcast.273, s32[2,288,1]{2,1,0:T(8,128)S(1)} %copy.156.dec_ref, ...), custom_call_target="tpu_custom_call" | custom-call | flops 1811939328 | bytes 8060928 | tf_op jit(solution)/shard_map/cross_forward/pallas_call | solution.py:189
  189.7 33.5 %feed_forward.1 = (f32[576,768]{1,0:T(8,128)}, bf16[16,2,48,3072]{3,2,1,0:T(8,128)(2,1)}, f32[576,768]{1,0:T(8,128)}, bf16[576,768]{1,0:T(8,128)(2,1)}, bf16[2,8...) custom-call(s32[1]{0:T(128)} %bitcast.refs_0_.up_ref, ...), custom_call_target="tpu_custom_call" | custom-call | flops 16307453952 | bytes 17694720 | tf_op jit(solution)/shard_map/feed_forward/pallas_call | solution.py:463
  225.5 29.2 %cross_backward.1 = (bf16[2,288,768]{2,1,0:T(8,128)(2,1)S(1)}, bf16[2,1024,768]{2,1,0:T(8,128)(2,1)}, bf16[2,1024,768]{2,1,0:T(8,128)(2,1)}) custom-call(bf16[2,288,768]{2,1,0:T(8,128)(2,1)S(1)} %bitcast.267, bf16[2,1024,1536]{2,1,0:T(8,128)(2,1)} %bitcast.274, bf16[2,1024,1536]{2,1,0:T(8,128)(2,1)} %bitcast.275, s32[2,288,1]{2,1,0:T(8,128)S(1)} %copy.156.dec_ref, ...), custom_call_target="tpu_custom_call" | custom-call | flops 4529848320 | bytes 16121856 | tf_op jit(solution)/shard_map/cross_backward/pallas_call | solution.py:215
  255.7 9.7 %after_cross.1 = (f32[576,768]{1,0:T(8,128)}, bf16[576,768]{1,0:T(8,128)(2,1)}, bf16[2,8,48,768]{3,2,1,0:T(8,128)(2,1)}, bf16[2,8,48,768]{3,2,1,0:T(8,128)(2,1)}, f32[1,768]{1,0:T(1,128)}) custom-call(s32[1]{0:T(128)} %bitcast.refs_0_.up_ref, bf16[576,768]{1,0:T(8,128)(2,1)} %bitcast.271, bf16[576,768]{1,0:T(8,128)(2,1)} %get-tuple-element.76.n_ref, ...), custom_call_target="tpu_custom_call" | custom-call | flops 2717908992 | bytes 15335424 | tf_op jit(solution)/shard_map/after_cross/pallas_call | solution.py:497
  266.6 23.6 %self_backward.1 = (bf16[2,288,768]{2,1,0:T(8,128)(2,1)S(1)}, bf16[2,288,768]{2,1,0:T(8,128)(2,1)S(1)}, bf16[2,288,768]{2,1,0:T(8,128)(2,1)S(1)}, f32[6,2,384]{2,1,0:T(2,128)S(1)}) custom-call(bf16[2,288,2304]{2,1,0:T(8,128)(2,1)} %bitcast.252, bf16[2,288,2304]{2,1,0:T(8,128)(2,1)} %bitcast.253, bf16[2,288,2304]{2,1,0:T(8,128)(2,1)} %bitcast.254, ...), custom_call_target="tpu_custom_call" | custom-call | flops 1698693120 | bytes 7077888 | tf_op jit(solution)/shard_map/self_backward/pallas_call | solution.py:272
  293.9 7.4 %input_back.1 = (bf16[576,768]{1,0:T(8,128)(2,1)}, f32[1,768]{1,0:T(1,128)}) custom-call(s32[1]{0:T(128)} %bitcast.refs_0_.up_ref, bf16[576,768]{1,0:T(8,128)(2,1)} %bitcast.258, bf16[576,768]{1,0:T(8,128)(2,1)} %bitcast.260, bf16[576,768]{1,0:T(8,128)(2,1)} %bitcast.262, bf16[576,768]{1,0:T(8,128)(2,1)} %bitcast.287, f32[576,768]{1,0:T(8,128)} %get-tuple-element.82.gh_ref, ...), custom_call_target="tpu_custom_call" | custom-call | flops 2038431744 | bytes 9732096 | tf_op jit(solution)/shard_map/input_back/pallas_call | solution.py:557
  309.1 10.3 %memory_outer.1 = (bf16[2,8,48,768]{3,2,1,0:T(8,128)(2,1)}, bf16[2,8,48,768]{3,2,1,0:T(8,128)(2,1)}) custom-call(s32[1]{0:T(128)} %bitcast.refs_0_.up_ref, bf16[2048,768]{1,0:T(8,128)(2,1)} %bitcast.293, bf16[2048,768]{1,0:T(8,128)(2,1)} %bitcast.326, bf16[2048,768]{1,0:T(8,128)(2,1)} %bitcast.328), custom_call_target="tpu_custom_call" | custom-call | flops 4831838208 | bytes 12976128 | tf_op jit(solution)/shard_map/memory_outer/pallas_call | solution.py:519
  319.5 11.6 %memory_back.1 = f32[2048,768]{1,0:T(8,128)} custom-call(s32[1]{0:T(128)} %bitcast.refs_0_.up_ref, bf16[2048,768]{1,0:T(8,128)(2,1)} %bitcast.327, bf16[2048,768]{1,0:T(8,128)(2,1)} %bitcast.329, bf16[768,1536]{1,0:T(8,128)(2,1)} %get-tuple-element.68.w_ref), custom_call_target="tpu_custom_call" | custom-call | flops 4831838208 | bytes 14942208 | tf_op jit(solution)/shard_map/memory_back/pallas_call | solution.py:537
  331.7 4.7 %collective-permute-start.43 = (f32[2688]{0:T(1024)S(1)}, f32[2688]{0:T(1024)S(1)}, u32[]{:S(2)}, u32[]{:S(2)}) collective-permute-start(f32[2688]{0:T(1024)S(1)} %add.220), channel_id=1, source_target_pairs={{0,16},{2,18},{4,20},{6,22},{8,24},{10,26},{12,28},{14,30},{16,0},... | collective-permute-start | bytes 32264 | tf_op jit(solution)/shard_map/ppermute | solution.py:612
  336.4 6.9 %self_outer.1 = (bf16[2,8,48,1152]{3,2,1,0:T(8,128)(2,1)}, bf16[2,8,48,1152]{3,2,1,0:T(8,128)(2,1)}) custom-call(s32[1]{0:T(128)} %bitcast.refs_0_.up_ref, bf16[576,768]{1,0:T(8,128)(2,1)} %get-tuple-element.86.x_ref, bf16[576,768]{1,0:T(8,128)(2,1)} %bitcast.259, bf16[576,768]{1,0:T(8,128)(2,1)} %bitcast.261, bf16[576,768]{1,0:T(8,128)(2,1)} %bitcast.263), custom_call_target="tpu_custom_call" | custom-call | flops 2038431744 | bytes 8257536 | tf_op jit(solution)/shard_map/self_outer/pallas_call | solution.py:519
  360.9 14.5 %collective-permute-done.30 = bf16[2,4,48,896]{3,2,1,0:T(8,128)(2,1)S(1)} collective-permute-done((bf16[2,4,48,896]{3,2,1,0:T(8,128)(2,1)S(1)}, bf16[2,4,48,896]{3,2,1,0:T(8,128)(2,1)S(1)}, u32[]{:S(2)}, u32[]{:S(2)}) %collective-permute-start.30) | collective-permute-done | bytes 688160 | tf_op jit(solution)/shard_map/ppermute | solution.py:612
  377.3 6.9 %collective-permute-done.19 = bf16[1,8,48,512]{3,2,1,0:T(8,128)(2,1)S(1)} collective-permute-done((bf16[1,8,48,512]{3,2,1,0:T(8,128)(2,1)S(1)}, bf16[1,8,48,512]{3,2,1,0:T(8,128)(2,1)S(1)}, u32[]{:S(2)}, u32[]{:S(2)}) %collective-permute-start.19) | collective-permute-done | bytes 393248 | tf_op jit(solution)/shard_map/ppermute | solution.py:616
  384.6 6.5 %collective-permute-done.31 = bf16[1,4,48,896]{3,2,1,0:T(8,128)(2,1)S(1)} collective-permute-done((bf16[1,4,48,896]{3,2,1,0:T(8,128)(2,1)S(1)}, bf16[1,4,48,896]{3,2,1,0:T(8,128)(2,1)S(1)}, u32[]{:S(2)}, u32[]{:S(2)}) %collective-permute-start.31) | collective-permute-done | bytes 344096 | tf_op jit(solution)/shard_map/ppermute | solution.py:616
  392.2 6.0 %collective-permute-done.20 = bf16[1,4,48,512]{3,2,1,0:T(8,128)(2,1)S(1)} collective-permute-done((bf16[1,4,48,512]{3,2,1,0:T(8,128)(2,1)S(1)}, bf16[1,4,48,512]{3,2,1,0:T(8,128)(2,1)S(1)}, u32[]{:S(2)}, u32[]{:S(2)}) %collective-permute-start.20) | collective-permute-done | bytes 196640 | tf_op jit(solution)/shard_map/ppermute | solution.py:612
  401.4 7.4 %collective-permute-done.23 = bf16[1,2,48,1152]{3,2,1,0:T(8,128)(2,1)S(1)} collective-permute-done((bf16[1,2,48,1152]{3,2,1,0:T(8,128)(2,1)S(1)}, bf16[1,2,48,1152]{3,2,1,0:T(8,128)(2,1)S(1)}, u32[]{:S(2)}, u32[]{:S(2)}) %collective-permute-start.23) | collective-permute-done | bytes 221216 | tf_op jit(solution)/shard_map/ppermute | solution.py:612
  409.0 6.4 %collective-permute-done.32 = bf16[1,2,48,1920]{3,2,1,0:T(8,128)(2,1)S(1)} collective-permute-done((bf16[1,2,48,1920]{3,2,1,0:T(8,128)(2,1)S(1)}, bf16[1,2,48,1920]{3,2,1,0:T(8,128)(2,1)S(1)}, u32[]{:S(2)}, u32[]{:S(2)}) %collective-permute-start.32) | collective-permute-done | bytes 368672 | tf_op jit(solution)/shard_map/ppermute | solution.py:612
  418.6 5.1 %collective-permute-done.33 = bf16[1,1,48,1920]{3,2,1,0:T(8,128)(2,1)S(1)} collective-permute-done((bf16[1,1,48,1920]{3,2,1,0:T(8,128)(2,1)S(1)}, bf16[1,1,48,1920]{3,2,1,0:T(8,128)(2,1)S(1)}, u32[]{:S(2)}, u32[]{:S(2)}) %collective-permute-start.33) | collective-permute-done | bytes 184352 | tf_op jit(solution)/shard_map/ppermute | solution.py:612
  (311 shorter events, 123.8 us)
Async XLA Ops:
  7.2 182.5 %all-gather.2.cloned.1.call-start = ((), (), s32[]{:S(2)}) async-start(), calls=%async_computation.1 | async-start | bytes 9732096 | tf_op jit(solution)/shard_map/all_gather | solution.py:782
  11.1 414.7 %reduce-scatter.2.cloned.1.call-start = ((), (), s32[]{:S(2)}) async-start(), calls=%async_computation.2 | async-start | bytes 9732096 | tf_op jit(solution)/shard_map/reduce_scatter | solution.py:849
  11.3 15.2 %collective-permute-start.9 = (bf16[1,1,48,1536]{3,2,1,0:T(8,128)(2,1)S(1)}, bf16[1,1,48,1536]{3,2,1,0:T(8,128)(2,1)S(1)}, u32[]{:S(2)}, u32[]{:S(2)}) collective-permute-start(bf16[1,1,48,1536]{3,2,1,0:T(8,128)(2,1)S(1)} %get-tuple-element.210), channel_id=1, source_target_pairs={{0,16},{2,18},{4,20},{6,22},{8,24},{10,26},{12,28},{14,30},{16,0},... | collective-permute-start | bytes 442376 | tf_op jit(solution)/shard_map/ppermute | solution.py:612
  15.4 17.0 %collective-permute-start = (bf16[1,1,48,1536]{3,2,1,0:T(8,128)(2,1)S(1)}, bf16[1,1,48,1536]{3,2,1,0:T(8,128)(2,1)S(1)}, u32[]{:S(2)}, u32[]{:S(2)}) collective-permute-start(bf16[1,1,48,1536]{3,2,1,0:T(8,128)(2,1)S(1)} %get-tuple-element.212), channel_id=1, source_target_pairs={{0,16},{2,18},{4,20},{6,22},{8,24},{10,26},{12,28},{14,30},{16,0},... | collective-permute-start | bytes 442376 | tf_op jit(solution)/shard_map/ppermute | solution.py:612
  26.5 14.9 %collective-permute-start.10 = (bf16[1,2,48,1536]{3,2,1,0:T(8,128)(2,1)S(1)}, bf16[1,2,48,1536]{3,2,1,0:T(8,128)(2,1)S(1)}, u32[]{:S(2)}, u32[]{:S(2)}) collective-permute-start(bf16[1,2,48,1536]{3,2,1,0:T(8,128)(2,1)S(1)} %maximum_select_fusion.8), channel_id=1, source_target_pairs={{0,8},{2,10},{4,12},{6,14},{8,0},{10,2},{12,4},{14,6},{16,24},{18,... | collective-permute-start | bytes 884744 | tf_op jit(solution)/shard_map/ppermute | solution.py:612
  32.5 16.7 %collective-permute-start.1 = (bf16[1,2,48,1536]{3,2,1,0:T(8,128)(2,1)S(1)}, bf16[1,2,48,1536]{3,2,1,0:T(8,128)(2,1)S(1)}, u32[]{:S(2)}, u32[]{:S(2)}) collective-permute-start(bf16[1,2,48,1536]{3,2,1,0:T(8,128)(2,1)S(1)} %maximum_select_fusion.7), channel_id=1, source_target_pairs={{0,8},{2,10},{4,12},{6,14},{8,0},{10,2},{12,4},{14,6},{16,24},{18,... | collective-permute-start | bytes 884744 | tf_op jit(solution)/shard_map/ppermute | solution.py:612
  41.6 14.9 %collective-permute-start.14 = (bf16[1,4,48,768]{3,2,1,0:T(8,128)(2,1)S(1)}, bf16[1,4,48,768]{3,2,1,0:T(8,128)(2,1)S(1)}, u32[]{:S(2)}, u32[]{:S(2)}) collective-permute-start(bf16[1,4,48,768]{3,2,1,0:T(8,128)(2,1)S(1)} %get-tuple-element.194), channel_id=1, source_target_pairs={{0,1},{1,0},{2,3},{3,2},{4,5},{5,4},{6,7},{7,6},{8,9},{9,8},{10,11... | collective-permute-start | bytes 884744 | tf_op jit(solution)/shard_map/ppermute | solution.py:616
  43.3 16.1 %collective-permute-start.11 = (bf16[1,4,48,768]{3,2,1,0:T(8,128)(2,1)S(1)}, bf16[1,4,48,768]{3,2,1,0:T(8,128)(2,1)S(1)}, u32[]{:S(2)}, u32[]{:S(2)}) collective-permute-start(bf16[1,4,48,768]{3,2,1,0:T(8,128)(2,1)S(1)} %get-tuple-element.196), channel_id=1, source_target_pairs={{0,4},{2,6},{4,0},{6,2},{8,12},{10,14},{12,8},{14,10},{16,20},{18,... | collective-permute-start | bytes 884744 | tf_op jit(solution)/shard_map/ppermute | solution.py:612
  50.1 16.3 %collective-permute-start.5 = (bf16[1,4,48,768]{3,2,1,0:T(8,128)(2,1)S(1)}, bf16[1,4,48,768]{3,2,1,0:T(8,128)(2,1)}, u32[]{:S(2)}, u32[]{:S(2)}) collective-permute-start(bf16[1,4,48,768]{3,2,1,0:T(8,128)(2,1)S(1)} %get-tuple-element.199), channel_id=1, source_target_pairs={{0,1},{1,0},{2,3},{3,2},{4,5},{5,4},{6,7},{7,6},{8,9},{9,8},{10,11... | collective-permute-start | bytes 884744 | tf_op jit(solution)/shard_map/ppermute | solution.py:616
  57.4 31.5 %collective-permute-start.15 = (bf16[2,4,48,768]{3,2,1,0:T(8,128)(2,1)}, bf16[2,4,48,768]{3,2,1,0:T(8,128)(2,1)}, u32[]{:S(2)}, u32[]{:S(2)}) collective-permute-start(bf16[2,4,48,768]{3,2,1,0:T(8,128)(2,1)} %get-tuple-element.192), channel_id=1, source_target_pairs={{0,4},{2,6},{4,0},{6,2},{8,12},{10,14},{12,8},{14,10},{16,20},{18,... | collective-permute-start | bytes 1769480 | tf_op jit(solution)/shard_map/ppermute | solution.py:612
  58.8 24.6 %collective-permute-start.2 = (bf16[1,4,48,768]{3,2,1,0:T(8,128)(2,1)}, bf16[1,4,48,768]{3,2,1,0:T(8,128)(2,1)}, u32[]{:S(2)}, u32[]{:S(2)}) collective-permute-start(bf16[1,4,48,768]{3,2,1,0:T(8,128)(2,1)} %get-tuple-element.201), channel_id=1, source_target_pairs={{0,4},{2,6},{4,0},{6,2},{8,12},{10,14},{12,8},{14,10},{16,20},{18,... | collective-permute-start | bytes 884744 | tf_op jit(solution)/shard_map/ppermute | solution.py:612
  60.4 30.1 %collective-permute-start.12 = (bf16[1,8,48,768]{3,2,1,0:T(8,128)(2,1)}, bf16[1,8,48,768]{3,2,1,0:T(8,128)(2,1)}, u32[]{:S(2)}, u32[]{:S(2)}) collective-permute-start(bf16[1,8,48,768]{3,2,1,0:T(8,128)(2,1)} %bitcast.33), channel_id=1, source_target_pairs={{0,1},{1,0},{2,3},{3,2},{4,5},{5,4},{6,7},{7,6},{8,9},{9,8},{10,11... | collective-permute-start | bytes 1769480 | tf_op jit(solution)/shard_map/ppermute | solution.py:616
  68.3 35.2 %collective-permute-start.6 = (bf16[2,4,48,768]{3,2,1,0:T(8,128)(2,1)}, bf16[2,4,48,768]{3,2,1,0:T(8,128)(2,1)}, u32[]{:S(2)}, u32[]{:S(2)}) collective-permute-start(bf16[2,4,48,768]{3,2,1,0:T(8,128)(2,1)} %get-tuple-element.197), channel_id=1, source_target_pairs={{0,4},{2,6},{4,0},{6,2},{8,12},{10,14},{12,8},{14,10},{16,20},{18,... | collective-permute-start | bytes 1769480 | tf_op jit(solution)/shard_map/ppermute | solution.py:612
  85.4 22.2 %collective-permute-start.3 = (bf16[1,8,48,768]{3,2,1,0:T(8,128)(2,1)}, bf16[1,8,48,768]{3,2,1,0:T(8,128)(2,1)}, u32[]{:S(2)}, u32[]{:S(2)}) collective-permute-start(bf16[1,8,48,768]{3,2,1,0:T(8,128)(2,1)} %bitcast.15), channel_id=1, source_target_pairs={{0,1},{1,0},{2,3},{3,2},{4,5},{5,4},{6,7},{7,6},{8,9},{9,8},{10,11... | collective-permute-start | bytes 1769480 | tf_op jit(solution)/shard_map/ppermute | solution.py:616
  88.9 26.1 %collective-permute-start.8 = (f32[32,6]{0,1:T(8,128)S(1)}, f32[32,6]{0,1:T(8,128)}, u32[]{:S(2)}, u32[]{:S(2)}) collective-permute-start(f32[32,6]{0,1:T(8,128)S(1)} %copy-done.38), channel_id=1, source_target_pairs={{0,1},{1,0},{2,3},{3,2},{4,5},{5,4},{6,7},{7,6},{8,9},{9,8},{10,11... | collective-permute-start | bytes 2312 | tf_op jit(solution)/shard_map/ppermute | solution.py:616
  90.4 26.1 %collective-permute-start.16 = (bf16[2,8,48,768]{3,2,1,0:T(8,128)(2,1)S(1)}, bf16[2,8,48,768]{3,2,1,0:T(8,128)(2,1)}, u32[]{:S(2)}, u32[]{:S(2)}) collective-permute-start(bf16[2,8,48,768]{3,2,1,0:T(8,128)(2,1)S(1)} %bitcast.283), channel_id=1, source_target_pairs={{0,2},{2,0},{4,6},{6,4},{8,10},{10,8},{12,14},{14,12},{16,18},{18,... | collective-permute-start | bytes 3538952 | tf_op jit(solution)/shard_map/ppermute | solution.py:612
  93.3 23.2 %collective-permute-start.13 = (bf16[2,8,48,768]{3,2,1,0:T(8,128)(2,1)}, bf16[2,8,48,768]{3,2,1,0:T(8,128)(2,1)}, u32[]{:S(2)}, u32[]{:S(2)}) collective-permute-start(bf16[2,8,48,768]{3,2,1,0:T(8,128)(2,1)} %pad_maximum_fusion.2.refs_1_), channel_id=1, source_target_pairs={{0,2},{2,0},{4,6},{6,4},{8,10},{10,8},{12,14},{14,12},{16,18},{18,... | collective-permute-start | bytes 3538952 | tf_op jit(solution)/shard_map/ppermute | solution.py:612
  106.0 17.5 %collective-permute-start.7 = (bf16[2,8,48,768]{3,2,1,0:T(8,128)(2,1)}, bf16[2,8,48,768]{3,2,1,0:T(8,128)(2,1)}, u32[]{:S(2)}, u32[]{:S(2)}) collective-permute-start(bf16[2,8,48,768]{3,2,1,0:T(8,128)(2,1)} %bitcast.18.refs_3_), channel_id=1, source_target_pairs={{0,2},{2,0},{4,6},{6,4},{8,10},{10,8},{12,14},{14,12},{16,18},{18,... | collective-permute-start | bytes 3538952 | tf_op jit(solution)/shard_map/ppermute | solution.py:612
  110.0 13.6 %collective-permute-start.4 = (bf16[2,8,48,768]{3,2,1,0:T(8,128)(2,1)}, bf16[2,8,48,768]{3,2,1,0:T(8,128)(2,1)}, u32[]{:S(2)}, u32[]{:S(2)}) collective-permute-start(bf16[2,8,48,768]{3,2,1,0:T(8,128)(2,1)} %pad_maximum_fusion.1.refs_1_), channel_id=1, source_target_pairs={{0,2},{2,0},{4,6},{6,4},{8,10},{10,8},{12,14},{14,12},{16,18},{18,... | collective-permute-start | bytes 3538952 | tf_op jit(solution)/shard_map/ppermute | solution.py:612
  306.1 41.3 %collective-permute-start.25 = (bf16[2,8,48,384]{3,2,1,0:T(8,128)(2,1)}, bf16[2,8,48,384]{3,2,1,0:T(8,128)(2,1)S(1)}, u32[]{:S(2)}, u32[]{:S(2)}) collective-permute-start(bf16[2,8,48,384]{3,2,1,0:T(8,128)(2,1)} %get-tuple-element.90), channel_id=1, source_target_pairs={{0,2},{2,0},{4,6},{6,4},{8,10},{10,8},{12,14},{14,12},{16,18},{18,... | collective-permute-start | bytes 1769480 | tf_op jit(solution)/shard_map/ppermute | solution.py:612
  306.6 43.1 %collective-permute-start.17 = (bf16[2,288,768]{2,1,0:T(8,128)(2,1)}, bf16[2,288,768]{2,1,0:T(8,128)(2,1)}, u32[]{:S(2)}, u32[]{:S(2)}) collective-permute-start(bf16[2,288,768]{2,1,0:T(8,128)(2,1)} %bitcast.309), channel_id=1, source_target_pairs={{0,1},{1,0},{2,3},{3,2},{4,5},{5,4},{6,7},{7,6},{8,9},{9,8},{10,11... | collective-permute-start | bytes 2654216 | tf_op jit(solution)/shard_map/ppermute | solution.py:616
  331.1 22.6 %collective-permute-start.26 = (bf16[2,8,48,768]{3,2,1,0:T(8,128)(2,1)}, bf16[2,8,48,768]{3,2,1,0:T(8,128)(2,1)}, u32[]{:S(2)}, u32[]{:S(2)}) collective-permute-start(bf16[2,8,48,768]{3,2,1,0:T(8,128)(2,1)} %get-tuple-element.92), channel_id=1, source_target_pairs={{0,2},{2,0},{4,6},{6,4},{8,10},{10,8},{12,14},{14,12},{16,18},{18,... | collective-permute-start | bytes 3538952 | tf_op jit(solution)/shard_map/ppermute | solution.py:612
  331.2 24.9 %collective-permute-start.29 = (bf16[2,8,48,768]{3,2,1,0:T(8,128)(2,1)}, bf16[2,8,48,768]{3,2,1,0:T(8,128)(2,1)S(1)}, u32[]{:S(2)}, u32[]{:S(2)}) collective-permute-start(bf16[2,8,48,768]{3,2,1,0:T(8,128)(2,1)} %get-tuple-element.94), channel_id=1, source_target_pairs={{0,2},{2,0},{4,6},{6,4},{8,10},{10,8},{12,14},{14,12},{16,18},{18,... | collective-permute-start | bytes 3538952 | tf_op jit(solution)/shard_map/ppermute | solution.py:612
  343.3 14.1 %collective-permute-start.18 = (bf16[2,8,48,1152]{3,2,1,0:T(8,128)(2,1)}, bf16[2,8,48,1152]{3,2,1,0:T(8,128)(2,1)S(1)}, u32[]{:S(2)}, u32[]{:S(2)}) collective-permute-start(bf16[2,8,48,1152]{3,2,1,0:T(8,128)(2,1)} %get-tuple-element.88), channel_id=1, source_target_pairs={{0,2},{2,0},{4,6},{6,4},{8,10},{10,8},{12,14},{14,12},{16,18},{18,... | collective-permute-start | bytes 5308424 | tf_op jit(solution)/shard_map/ppermute | solution.py:612
  355.4 21.4 %collective-permute-start.27 = (bf16[1,8,48,1024]{3,2,1,0:T(8,128)(2,1)S(1)}, bf16[1,8,48,1024]{3,2,1,0:T(8,128)(2,1)S(1)}, u32[]{:S(2)}, u32[]{:S(2)}) collective-permute-start(bf16[1,8,48,1024]{3,2,1,0:T(8,128)(2,1)S(1)} %pad_maximum_fusion.3), channel_id=1, source_target_pairs={{0,1},{1,0},{2,3},{3,2},{4,5},{5,4},{6,7},{7,6},{8,9},{9,8},{10,11... | collective-permute-start | bytes 2359304 | tf_op jit(solution)/shard_map/ppermute | solution.py:616
  357.1 18.3 %collective-permute-start.30 = (bf16[2,4,48,896]{3,2,1,0:T(8,128)(2,1)S(1)}, bf16[2,4,48,896]{3,2,1,0:T(8,128)(2,1)S(1)}, u32[]{:S(2)}, u32[]{:S(2)}) collective-permute-start(bf16[2,4,48,896]{3,2,1,0:T(8,128)(2,1)S(1)} %select_bitcast_fusion), channel_id=1, source_target_pairs={{0,4},{2,6},{4,0},{6,2},{8,12},{10,14},{12,8},{14,10},{16,20},{18,... | collective-permute-start | bytes 2064392 | tf_op jit(solution)/shard_map/ppermute | solution.py:612
  359.1 25.1 %collective-permute-start.19 = (bf16[1,8,48,512]{3,2,1,0:T(8,128)(2,1)S(1)}, bf16[1,8,48,512]{3,2,1,0:T(8,128)(2,1)S(1)}, u32[]{:S(2)}, u32[]{:S(2)}) collective-permute-start(bf16[1,8,48,512]{3,2,1,0:T(8,128)(2,1)S(1)} %slice.289), channel_id=1, source_target_pairs={{0,1},{1,0},{2,3},{3,2},{4,5},{5,4},{6,7},{7,6},{8,9},{9,8},{10,11... | collective-permute-start | bytes 1179656 | tf_op jit(solution)/shard_map/ppermute | solution.py:616
  360.1 31.1 %collective-permute-start.21 = (bf16[2,4,48,640]{3,2,1,0:T(8,128)(2,1)S(1)}, bf16[2,4,48,640]{3,2,1,0:T(8,128)(2,1)S(1)}, u32[]{:S(2)}, u32[]{:S(2)}) collective-permute-start(bf16[2,4,48,640]{3,2,1,0:T(8,128)(2,1)S(1)} %select_bitcast_fusion.1), channel_id=1, source_target_pairs={{0,4},{2,6},{4,0},{6,2},{8,12},{10,14},{12,8},{14,10},{16,20},{18,... | collective-permute-start | bytes 1474568 | tf_op jit(solution)/shard_map/ppermute | solution.py:612
  375.7 15.4 %collective-permute-start.31 = (bf16[1,4,48,896]{3,2,1,0:T(8,128)(2,1)S(1)}, bf16[1,4,48,896]{3,2,1,0:T(8,128)(2,1)S(1)}, u32[]{:S(2)}, u32[]{:S(2)}) collective-permute-start(bf16[1,4,48,896]{3,2,1,0:T(8,128)(2,1)S(1)} %slice.306), channel_id=1, source_target_pairs={{0,1},{1,0},{2,3},{3,2},{4,5},{5,4},{6,7},{7,6},{8,9},{9,8},{10,11... | collective-permute-start | bytes 1032200 | tf_op jit(solution)/shard_map/ppermute | solution.py:616
  377.0 21.2 %collective-permute-start.28 = (bf16[1,4,48,1024]{3,2,1,0:T(8,128)(2,1)S(1)}, bf16[1,4,48,1024]{3,2,1,0:T(8,128)(2,1)S(1)}, u32[]{:S(2)}, u32[]{:S(2)}) collective-permute-start(bf16[1,4,48,1024]{3,2,1,0:T(8,128)(2,1)S(1)} %select_bitcast_fusion.2), channel_id=1, source_target_pairs={{0,4},{2,6},{4,0},{6,2},{8,12},{10,14},{12,8},{14,10},{16,20},{18,... | collective-permute-start | bytes 1179656 | tf_op jit(solution)/shard_map/ppermute | solution.py:612
  384.3 13.8 %collective-permute-start.20 = (bf16[1,4,48,512]{3,2,1,0:T(8,128)(2,1)S(1)}, bf16[1,4,48,512]{3,2,1,0:T(8,128)(2,1)S(1)}, u32[]{:S(2)}, u32[]{:S(2)}) collective-permute-start(bf16[1,4,48,512]{3,2,1,0:T(8,128)(2,1)S(1)} %select_bitcast_fusion.5), channel_id=1, source_target_pairs={{0,4},{2,6},{4,0},{6,2},{8,12},{10,14},{12,8},{14,10},{16,20},{18,... | collective-permute-start | bytes 589832 | tf_op jit(solution)/shard_map/ppermute | solution.py:612
  399.4 16.0 %collective-permute-start.32 = (bf16[1,2,48,1920]{3,2,1,0:T(8,128)(2,1)S(1)}, bf16[1,2,48,1920]{3,2,1,0:T(8,128)(2,1)S(1)}, u32[]{:S(2)}, u32[]{:S(2)}) collective-permute-start(bf16[1,2,48,1920]{3,2,1,0:T(8,128)(2,1)S(1)} %select_bitcast_fusion.3), channel_id=1, source_target_pairs={{0,8},{2,10},{4,12},{6,14},{8,0},{10,2},{12,4},{14,6},{16,24},{18,... | collective-permute-start | bytes 1105928 | tf_op jit(solution)/shard_map/ppermute | solution.py:612
  (66 other events, 420.7 us)
Sparse Core Ops, SparseCore 0:
  11.5 109.0 all-gather.1
  223.3 139.5 reduce-scatter.1
